TPU v7x, 32 devices: a whole 2x2x4 slice. The times are simulated.
32 devices in a mesh: dp: 4 (over z), ctx: 4 (over y, core), tp: 2 (over x).
Axes of the slice: x: 2, y: 2, z: 4, core: 2. Of those that a mesh axis runs over, the one named last changes fastest.
Arguments:
- tokens: bfloat16 [4, 4096, 1024], P('dp', 'ctx'), may hold values from -6 to 6
- lengths: int32 [4], replicated, may hold values from 1 to 1024, as said below
- norm_gain: bfloat16 [2, 1024], P(None, ('dp', 'ctx')), may hold values from 0.25 to 1.75
- norm_bias: bfloat16 [2, 1024], P(None, ('dp', 'ctx')), may hold values from -1.5 to 1.5
- qkv_weight: bfloat16 [1024, 3, 1024], P(('dp', 'ctx'), None, 'tp'), may hold values from -0.1875 to 0.1875
- qv_bias: float32 [2, 1024], P(None, 'tp'), may hold values from -1.5 to 1.5
- out_weight: bfloat16 [1024, 1024], P('tp', ('dp', 'ctx')), may hold values from -2.5 to 2.5
- mlp_in: bfloat16 [1024, 4096], P(('dp', 'ctx'), 'tp'), may hold values from -0.1875 to 0.1875
- mlp_bias: float32 [4096], P('tp'), may hold values from -1.5 to 1.5
- mlp_out: bfloat16 [4096, 1024], P('tp', ('dp', 'ctx')), may hold values from -0.125 to 0.125
- out_bias: bfloat16 [2, 1024], P(None, ('dp', 'ctx')), may hold values from -1.5 to 1.5
- cotangent: bfloat16 [4, 4096, 1024], P('dp', 'ctx'), may hold values from -6 to 6
Outputs:
- result: bfloat16 [4, 4096, 1024], P('dp', 'ctx')
- grad_tokens: bfloat16 [4, 4096, 1024], P('dp', 'ctx')
- grad_norm_gain: float32 [2, 1024], P(None, ('dp', 'ctx'))
- grad_norm_bias: float32 [2, 1024], P(None, ('dp', 'ctx'))
- grad_qkv_weight: float32 [1024, 3, 1024], P(('dp', 'ctx'), None, 'tp')
- grad_qv_bias: float32 [2, 1024], P(None, 'tp')
- grad_out_weight: float32 [1024, 1024], P('tp', ('dp', 'ctx'))
- grad_mlp_in: float32 [1024, 4096], P(('dp', 'ctx'), 'tp')
- grad_mlp_bias: float32 [4096], P('tp')
- grad_mlp_out: float32 [4096, 1024], P('tp', ('dp', 'ctx'))
- grad_out_bias: float32 [2, 1024], P(None, ('dp', 'ctx'))
Inputs may be any that keep to these rules, and one draw needn't show every extreme that they name: `lengths`: entry c counts the live tokens at the start of context device c's block of 1024 slots of every image; the entries sum to 3072, every entry is at least 1, and exactly one entry is 1024.
All inputs are finite; a program needn't handle non-finite values.
Results may differ from a plain program's by a relative error of at most 0.02.
Values may be sent and summed in bfloat16 or wider, within the bound.
No kernel may reach another device: no remote copies, remote signals or barrier semaphores. Data moves between devices by JAX's collectives and lax.ppermute only.
A program may use at most 384 MiB of HBM per device.

v0:
```python
import math

import jax
import jax.numpy as jnp
from jax import lax
from jax.sharding import PartitionSpec as P

HD = 64


NEG = -1e30
EPS = 1e-06


def normalize(values, gain, shift):
    mean = jnp.mean(values, axis=-1, keepdims=True)
    centred = values - mean
    var = jnp.mean(centred * centred, axis=-1, keepdims=True)
    return centred * lax.rsqrt(var + EPS) * gain + shift


def gelu_exact(values):
    return jax.nn.gelu(values, approximate=False)


def slot_live(positions, lengths, cap):
    owner = positions // cap
    ctx_ids = lax.iota(jnp.int32, lengths.shape[0])
    limit = jnp.sum(jnp.where(owner[:, None] == ctx_ids[None, :], lengths[None, :], 0), axis=1)
    return positions % cap < limit


def body(
    tokens,
    lengths,
    norm_gain,
    norm_bias,
    qkv_weight,
    qv_bias,
    out_weight,
    mlp_in,
    mlp_bias,
    mlp_out,
    out_bias,
    cotangent,
):
    images, cap, width = tokens.shape
    rows = images * cap
    n_ctx = lax.axis_size("ctx")
    slots = n_ctx * cap
    local_width = qkv_weight.shape[2]
    heads_here = local_width // HD
    factor = 1.0 / math.sqrt(HD)
    place = lax.axis_index("ctx")
    row_live = slot_live(place * cap + lax.iota(jnp.int32, cap), lengths, cap)
    live_col = jnp.tile(row_live.astype(jnp.float32), images)[:, None]
    key_live = slot_live(lax.iota(jnp.int32, slots), lengths, cap)
    shards = (qkv_weight, out_weight, mlp_in, mlp_out, norm_gain, norm_bias, out_bias)
    full = (
        lax.all_gather(shards[0], ("dp", "ctx"), axis=0, tiled=True),
        lax.all_gather(shards[1], ("dp", "ctx"), axis=1, tiled=True),
        lax.all_gather(shards[2], ("dp", "ctx"), axis=0, tiled=True),
        lax.all_gather(shards[3], ("dp", "ctx"), axis=1, tiled=True),
        lax.all_gather(shards[4], ("dp", "ctx"), axis=1, tiled=True),
        lax.all_gather(shards[5], ("dp", "ctx"), axis=1, tiled=True),
        lax.all_gather(shards[6], ("dp", "ctx"), axis=1, tiled=True),
    )
    w_qkv, w_out, w_in, w_down, gains, shifts, biases = full
    gain_f = gains.astype(jnp.float32)
    shift_f = shifts.astype(jnp.float32)
    bias_f = biases.astype(jnp.float32)
    x = tokens.reshape(rows, width).astype(jnp.float32)
    h1 = normalize(x, gain_f[0], shift_f[0]).astype(jnp.bfloat16)
    qkv = jnp.einsum("td,dke->tke", h1, w_qkv, preferred_element_type=jnp.float32)
    query = (qkv[:, 0] + qv_bias[0]).astype(jnp.bfloat16)
    key = qkv[:, 1].astype(jnp.bfloat16)
    value = (qkv[:, 2] + qv_bias[1]).astype(jnp.bfloat16)
    query_four = query.reshape(images, cap, heads_here, HD)
    key_three = key.reshape(images, cap, local_width)
    value_three = value.reshape(images, cap, local_width)
    peak = jnp.full((images, heads_here, cap), NEG, jnp.float32)
    key_piece = lax.all_gather(key_three, "ctx", axis=1, tiled=True)
    value_piece = lax.all_gather(value_three, "ctx", axis=1, tiled=True)
    count = key_piece.shape[1]
    usable = slot_live(lax.iota(jnp.int32, count), lengths, cap)
    key_four = key_piece.reshape(images, count, heads_here, HD)
    value_four = value_piece.reshape(images, count, heads_here, HD)
    score = (
        jnp.einsum("bqhd,bkhd->bhqk", query_four, key_four, preferred_element_type=jnp.float32)
        * factor
    )
    score = jnp.where(usable, score, NEG)
    top = jnp.maximum(peak, jnp.max(score, axis=-1))
    weight = jnp.where(usable, jnp.exp(score - top[..., None]), 0.0)
    total = jnp.sum(weight, axis=-1)
    accum = jnp.einsum(
        "bhqk,bkhd->bhqd",
        weight.astype(jnp.bfloat16),
        value_four,
        preferred_element_type=jnp.float32,
    )
    peak, total, accum = (top, total, accum)
    attn_f = accum / total[..., None]
    log_total = peak + jnp.log(total)
    attended = jnp.transpose(attn_f, (0, 2, 1, 3)).reshape(rows, local_width).astype(jnp.bfloat16)
    attn_part = jnp.dot(attended, w_out, preferred_element_type=jnp.float32)
    x_one = x + (lax.psum(attn_part.astype(jnp.bfloat16), "tp").astype(jnp.float32) + bias_f[0])
    h2 = normalize(x_one, gain_f[1], shift_f[1]).astype(jnp.bfloat16)
    pre = jnp.dot(h2, w_in, preferred_element_type=jnp.float32) + mlp_bias
    act = gelu_exact(pre).astype(jnp.bfloat16)
    down = (
        lax.psum(
            jnp.dot(act, w_down, preferred_element_type=jnp.float32).astype(jnp.bfloat16), "tp"
        ).astype(jnp.float32)
        + bias_f[1]
    )
    result = ((x_one + down) * live_col).astype(jnp.bfloat16).reshape(images, cap, width)
    w_qkv, w_out, w_in, w_down = (
        lax.all_gather(shards[0], ("dp", "ctx"), axis=0, tiled=True),
        lax.all_gather(shards[1], ("dp", "ctx"), axis=1, tiled=True),
        lax.all_gather(shards[2], ("dp", "ctx"), axis=0, tiled=True),
        lax.all_gather(shards[3], ("dp", "ctx"), axis=1, tiled=True),
        lax.all_gather(shards[4], ("dp", "ctx"), axis=1, tiled=True),
        lax.all_gather(shards[5], ("dp", "ctx"), axis=1, tiled=True),
        lax.all_gather(shards[6], ("dp", "ctx"), axis=1, tiled=True),
    )[:4]
    d_out = cotangent.reshape(rows, width).astype(jnp.float32) * live_col
    d_down = d_out.astype(jnp.bfloat16)
    bias_grad_down = jnp.sum(d_down.astype(jnp.float32), axis=0)
    grad_down = jnp.einsum("tf,td->fd", act, d_down, preferred_element_type=jnp.float32)
    d_act = jnp.einsum("td,fd->tf", d_down, w_down, preferred_element_type=jnp.float32)
    gelu_back = jax.vjp(gelu_exact, pre)[1]
    d_pre = gelu_back(d_act)[0].astype(jnp.bfloat16)
    mlp_bias_grad = jnp.sum(d_pre.astype(jnp.float32), axis=0)
    grad_in = jnp.einsum("td,tf->df", h2, d_pre, preferred_element_type=jnp.float32)
    mlp_back_part = jnp.einsum("tf,df->td", d_pre, w_in, preferred_element_type=jnp.float32)
    norm_back_two = jax.vjp(normalize, x_one, gain_f[1], shift_f[1])[1]
    d_x_norm, gain_grad_two, shift_grad_two = norm_back_two(
        lax.psum(mlp_back_part.astype(jnp.bfloat16), "tp").astype(jnp.float32)
    )
    d_x_one = d_out + d_x_norm
    d_branch = d_x_one.astype(jnp.bfloat16)
    bias_grad_attn = jnp.sum(d_branch.astype(jnp.float32), axis=0)
    grad_out = jnp.einsum("te,td->ed", attended, d_branch, preferred_element_type=jnp.float32)
    d_att = jnp.einsum("td,ed->te", d_branch, w_out, preferred_element_type=jnp.float32).astype(
        jnp.bfloat16
    )
    key_all, value_all = (
        lax.all_gather(key_three, "ctx", axis=1, tiled=True),
        lax.all_gather(value_three, "ctx", axis=1, tiled=True),
    )
    key_all = key_all.reshape(images, slots, heads_here, HD)
    value_all = value_all.reshape(images, slots, heads_here, HD)
    d_att_four = d_att.reshape(images, cap, heads_here, HD)
    delta = jnp.einsum("bqhd,bhqd->bhq", d_att_four.astype(jnp.float32), attn_f)
    score = (
        jnp.einsum("bqhd,bkhd->bhqk", query_four, key_all, preferred_element_type=jnp.float32)
        * factor
    )
    prob = jnp.where(key_live, jnp.exp(score - log_total[..., None]), 0.0)
    d_prob = jnp.einsum(
        "bqhd,bkhd->bhqk", d_att_four, value_all, preferred_element_type=jnp.float32
    )
    d_score = (prob * (d_prob - delta[..., None])).astype(jnp.bfloat16)
    d_query = (
        jnp.einsum("bhqk,bkhd->bqhd", d_score, key_all, preferred_element_type=jnp.float32) * factor
    )
    d_key_all = (
        jnp.einsum("bhqk,bqhd->bkhd", d_score, query_four, preferred_element_type=jnp.float32)
        * factor
    )
    d_value_all = jnp.einsum(
        "bhqk,bqhd->bkhd", prob.astype(jnp.bfloat16), d_att_four, preferred_element_type=jnp.float32
    )
    d_key, d_value = (
        lax.psum_scatter(
            d_key_all.reshape(images, slots, local_width).astype(jnp.bfloat16),
            "ctx",
            scatter_dimension=1,
            tiled=True,
        ).astype(jnp.float32),
        lax.psum_scatter(
            d_value_all.reshape(images, slots, local_width).astype(jnp.bfloat16),
            "ctx",
            scatter_dimension=1,
            tiled=True,
        ).astype(jnp.float32),
    )
    d_qkv = jnp.stack(
        [
            d_query.reshape(rows, local_width),
            d_key.reshape(rows, local_width),
            d_value.reshape(rows, local_width),
        ],
        axis=1,
    ).astype(jnp.bfloat16)
    d_qkv_sums = jnp.sum(d_qkv.astype(jnp.float32), axis=0)
    qv_grad = jnp.stack([d_qkv_sums[0], d_qkv_sums[2]])
    grad_qkv = jnp.einsum("td,tke->dke", h1, d_qkv, preferred_element_type=jnp.float32)
    attn_back_part = jnp.einsum("tke,dke->td", d_qkv, w_qkv, preferred_element_type=jnp.float32)
    norm_back_one = jax.vjp(normalize, x, gain_f[0], shift_f[0])[1]
    d_x_first, gain_grad_one, shift_grad_one = norm_back_one(
        lax.psum(attn_back_part.astype(jnp.bfloat16), "tp").astype(jnp.float32)
    )
    grad_tokens = (d_x_one + d_x_first).astype(jnp.bfloat16).reshape(images, cap, width)
    gain_stack = jnp.stack([gain_grad_one, gain_grad_two])
    shift_stack = jnp.stack([shift_grad_one, shift_grad_two])
    summed = (
        lax.psum_scatter(
            grad_qkv.astype(jnp.bfloat16), ("dp", "ctx"), scatter_dimension=0, tiled=True
        ).astype(jnp.float32),
        lax.psum_scatter(
            grad_out.astype(jnp.bfloat16), ("dp", "ctx"), scatter_dimension=1, tiled=True
        ).astype(jnp.float32),
        lax.psum_scatter(
            grad_in.astype(jnp.bfloat16), ("dp", "ctx"), scatter_dimension=0, tiled=True
        ).astype(jnp.float32),
        lax.psum_scatter(
            grad_down.astype(jnp.bfloat16), ("dp", "ctx"), scatter_dimension=1, tiled=True
        ).astype(jnp.float32),
        lax.psum_scatter(
            gain_stack.astype(jnp.bfloat16), ("dp", "ctx"), scatter_dimension=1, tiled=True
        ).astype(jnp.float32),
        lax.psum_scatter(
            shift_stack.astype(jnp.bfloat16), ("dp", "ctx"), scatter_dimension=1, tiled=True
        ).astype(jnp.float32),
        lax.psum_scatter(
            jnp.stack([bias_grad_attn, bias_grad_down]).astype(jnp.bfloat16),
            ("dp", "ctx"),
            scatter_dimension=1,
            tiled=True,
        ).astype(jnp.float32),
    )
    bias_summed = lax.psum((qv_grad, mlp_bias_grad), ("dp", "ctx"))
    return (
        result,
        grad_tokens,
        summed[4],
        summed[5],
        summed[0],
        bias_summed[0],
        summed[1],
        summed[2],
        bias_summed[1],
        summed[3],
        summed[6],
    )


def solution(mesh):
    in_specs = (
        P("dp", "ctx", None),
        P(),
        P(None, ("dp", "ctx")),
        P(None, ("dp", "ctx")),
        P(("dp", "ctx"), None, "tp"),
        P(None, "tp"),
        P("tp", ("dp", "ctx")),
        P(("dp", "ctx"), "tp"),
        P("tp"),
        P("tp", ("dp", "ctx")),
        P(None, ("dp", "ctx")),
        P("dp", "ctx", None),
    )
    out_specs = (
        P("dp", "ctx", None),
        P("dp", "ctx", None),
        P(None, ("dp", "ctx")),
        P(None, ("dp", "ctx")),
        P(("dp", "ctx"), None, "tp"),
        P(None, "tp"),
        P("tp", ("dp", "ctx")),
        P(("dp", "ctx"), "tp"),
        P("tp"),
        P("tp", ("dp", "ctx")),
        P(None, ("dp", "ctx")),
    )
    return jax.shard_map(body, mesh=mesh, in_specs=in_specs, out_specs=out_specs, check_vma=False)
```

profile of v0, /device:TPU:0, one launch (start us, length us, event | category | flops | bytes accessed | tf_op | source)
XLA Modules:
  0.0 1294.6 jit_solution(3122458870612302037)
XLA Ops:
  8.0 23.2 %all-gather.1 = bf16[16,64,2]{1,2,0:T(2,128)(2,1)S(1)} all-gather(bf16[1,64,2]{1,2,0:T(2,128)(2,1)} %bitcast.234), channel_id=1, replica_groups=mesh['dp'=4,'ctx'=4,'tp'=2] {'dp','ctx'}, dimensions={0}, use_global_device_ids=true | all-gather | bytes 4352 | tf_op jit(solution)/shard_map/all_gather | solution.py:64
  31.3 17.5 %all-gather.2 = bf16[16,64,2]{1,2,0:T(2,128)(2,1)S(1)} all-gather(bf16[1,64,2]{1,2,0:T(2,128)(2,1)} %bitcast.235), channel_id=1, replica_groups=mesh['dp'=4,'ctx'=4,'tp'=2] {'dp','ctx'}, dimensions={0}, use_global_device_ids=true | all-gather | bytes 4352 | tf_op jit(solution)/shard_map/all_gather | solution.py:65
  73.9 27.5 %all-gather.21.cloned.1.call-done = bf16[4096,1,512]{0,2,1:T(8,128)(2,1)} async-done(((bf16[1024,1,512]{0,2,1:T(8,128)(2,1)}), bf16[4096,1,512]{0,2,1:T(8,128)(2,1)}) %all-gather.21.cloned.1.call-update) | async-done | bytes 4194320 | tf_op jit(solution)/shard_map/all_gather | solution.py:82
  101.3 47.5 %select_reduce_fusion = (f32[8,1024]{1,0:T(8,128)S(1)}, f32[8,1024,4096]{2,1,0:T(8,128)}) fusion(pred[4096]{0:T(1024)(128)(4,1)S(1)} %fusion.50, bf16[4096,8,64]{0,2,1:T(8,128)(2,1)} %bitcast.187, f32[1024,8,64]{0,2,1:T(8,128)S(1)} %bitcast.190, f32[8,64]{1,0:T(8,128)S(1)} %add.197), kind=kOutput, calls=%fused_computation.3 | convolution fusion | flops 4396670976 | bytes 140548096 | tf_op jit(solution)/shard_map/bqhd,bkhd->bhqk/dot_general | solution.py:89
  148.9 41.5 %fusion.1 = f32[8,1024]{1,0:T(8,128)S(1)} fusion(f32[8,1024,4096]{2,1,0:T(8,128)} %get-tuple-element.38, f32[8,1024]{1,0:T(8,128)S(1)} %broadcast_maximum_fusion, pred[4096]{0:T(1024)(128)(4,1)S(1)} %fusion.50), kind=kLoop, calls=%fused_computation.5 | loop fusion | flops 167763968 | bytes 134287360 | tf_op jit(solution)/shard_map/reduce_sum | solution.py:95
  190.4 46.0 %fusion.91 = (bf16[8,1024,64]{1,2,0:T(8,128)(2,1)S(1)}, f32[8,1024,64]{1,2,0:T(8,128)}) fusion(f32[8,1024]{1,0:T(8,128)S(1)} %fusion.1, bf16[4096,8,64]{0,2,1:T(8,128)(2,1)} %bitcast.237, f32[8,1024,4096]{2,1,0:T(8,128)} %get-tuple-element.38, f32[8,1024]{1,0:T(8,128)S(1)} %broadcast_maximum_fusion, pred[4096]{0:T(1024)(128)(4,1)S(1)} %fusion.50), kind=kOutput, calls=%fused_computation.156 | convolution fusion | flops 4463788032 | bytes 141627392 | tf_op jit(solution)/shard_map/bhqk,bkhd->bhqd/dot_general | solution.py:96
  242.1 20.3 %all-gather.3 = bf16[16,64,2]{1,2,0:T(2,128)(2,1)S(1)} all-gather(bf16[1,64,2]{1,2,0:T(2,128)(2,1)S(1)} %bitcast.236), channel_id=1, replica_groups=mesh['dp'=4,'ctx'=4,'tp'=2] {'dp','ctx'}, dimensions={0}, use_global_device_ids=true | all-gather | bytes 4352 | tf_op jit(solution)/shard_map/all_gather | solution.py:66
  263.2 40.6 %all-reduce.6.cloned.1.call-done = bf16[1024,1024]{1,0:T(8,128)(2,1)} async-done(((bf16[1024,1024]{1,0:T(8,128)(2,1)}), bf16[1024,1024]{1,0:T(8,128)(2,1)}) %all-reduce.6.cloned.1.call-update) | async-done | bytes 2097168 | tf_op jit(solution)/shard_map/psum | solution.py:107
  307.4 49.2 %all-gather.17.cloned.1.call-done = bf16[1024,2048]{1,0:T(8,128)(2,1)} async-done(((bf16[64,2048]{1,0:T(8,128)(2,1)}), bf16[1024,2048]{1,0:T(8,128)(2,1)}) %all-gather.17.cloned.1.call-update) | async-done | bytes 4194320 | tf_op jit(solution)/shard_map/all_gather | solution.py:62
  356.6 28.6 %multiply_convert_fusion.2 = (bf16[1024,2048]{1,0:T(8,128)(2,1)}, f32[1024,2048]{1,0:T(8,128)}, f32[1024,2048]{1,0:T(8,128)}) fusion(f32[2048]{0:T(1024)S(1)} %copy-done.56, bf16[1024,2048]{1,0:T(8,128)(2,1)} %all-gather.17.cloned.1.call-done, f32[1024]{0:T(1024)S(1)} %bitcast.232, f32[1024]{0:T(1024)S(1)} %bitcast.211, f32[1024]{0:T(1024)S(1)} %fusion.64, ...), kind=kOutput, calls=%fused_computation.16 | convolution fusion | flops 4442816512 | bytes 29388800 | tf_op jit(solution)/shard_map/dot_general | solution.py:109
  385.3 22.8 %all-gather.19.cloned.1.call-done = bf16[2048,1024]{0,1:T(8,128)(2,1)} async-done(((bf16[2048,64]{0,1:T(8,128)(2,1)}), bf16[2048,1024]{0,1:T(8,128)(2,1)}) %all-gather.19.cloned.1.call-update) | async-done | bytes 4194320 | tf_op jit(solution)/shard_map/all_gather | solution.py:63
  431.8 61.3 %all-reduce.8.cloned.1.call-done = bf16[1024,1024]{1,0:T(8,128)(2,1)} async-done(((bf16[1024,1024]{1,0:T(8,128)(2,1)}), bf16[1024,1024]{1,0:T(8,128)(2,1)}) %all-reduce.8.cloned.1.call-update) | async-done | bytes 2097168 | tf_op jit(solution)/shard_map/psum | solution.py:139
  507.0 44.9 %fusion.15 = bf16[8,64,4096]{2,1,0:T(8,128)(2,1)} fusion(bf16[1024,8,64]{0,2,1:T(8,128)(2,1)S(1)} %bitcast.241, f32[8,1024,4096]{2,1,0:T(8,128)} %get-tuple-element.38, f32[8,1024]{1,0:T(8,128)S(1)} %log_add_fusion, pred[4096]{0:T(1024)(128)(4,1)S(1)} %fusion.50), kind=kOutput, calls=%fused_computation.33 | convolution fusion | flops 4431282176 | bytes 139497472 | tf_op jit(solution)/shard_map/bhqk,bqhd->bkhd/dot_general | solution.py:172
  558.5 78.3 %multiply_convert_fusion = bf16[8,1024,4096]{2,1,0:T(8,128)(2,1)} fusion(f32[8,1024,4096]{2,1,0:T(8,128)} %get-tuple-element.38, f32[8,1024]{1,0:T(8,128)S(1)} %get-tuple-element.42, f32[8,1024]{1,0:T(8,128)S(1)} %log_add_fusion, pred[4096]{0:T(1024)(128)(4,1)S(1)} %fusion.50, bf16[1024,8,64]{0,2,1:T(8,128)(2,1)S(1)} %bitcast.242, ...), kind=kOutput, calls=%fused_computation | convolution fusion | flops 4496293888 | bytes 206639104 | tf_op jit(solution)/shard_map/bqhd,bkhd->bhqk/dot_general | solution.py:161
  636.8 26.0 %multiply_convert_fusion.1 = bf16[8,64,4096]{2,1,0:T(8,128)(2,1)} fusion(bf16[8,1024,4096]{2,1,0:T(8,128)(2,1)} %multiply_convert_fusion, f32[1024,8,64]{0,2,1:T(8,128)S(1)} %bitcast.191, f32[8,64]{1,0:T(8,128)S(1)} %copy-done.14), kind=kOutput, calls=%fused_computation.14 | convolution fusion | flops 4300210176 | bytes 73402368 | tf_op jit(solution)/shard_map/bhqk,bqhd->bkhd/dot_general | solution.py:169
  679.0 28.2 %multiply_convert_fusion.4 = bf16[8,64,1024]{2,1,0:T(8,128)(2,1)S(1)} fusion(bf16[4096,8,64]{0,2,1:T(8,128)(2,1)S(1)} %bitcast.188, bf16[8,1024,4096]{2,1,0:T(8,128)(2,1)} %multiply_convert_fusion), kind=kOutput, calls=%fused_computation.81 | convolution fusion | flops 4296015872 | bytes 72351744 | tf_op jit(solution)/shard_map/bhqk,bkhd->bqhd/dot_general | solution.py:166
  748.4 81.6 %all-reduce.10.cloned.1.call-done = (bf16[1024,1024]{1,0:T(8,128)(2,1)}, bf16[1024,1024]{1,0:T(8,128)(2,1)}) async-done(((bf16[1024,1024]{1,0:T(8,128)(2,1)}, bf16[1024,1024]{1,0:T(8,128)(2,1)}), (bf16[1024,1024]{1,0:T(8,128)(2,1)}, bf16[1024,1024]{1,0:T(8,128)(2,1)})) %all-reduce.10.cloned.1.call-update) | async-done | bytes 4194320 | tf_op jit(solution)/shard_map/psum | solution.py:112
  846.7 43.0 %reduce-scatter.32.cloned.1.call-done = bf16[64,2]{1,0:T(8,128)(2,1)} async-done(((bf16[1024,2]{1,0:T(8,128)(2,1)}), bf16[64,2]{1,0:T(8,128)(2,1)}) %reduce-scatter.32.cloned.1.call-update) | async-done | bytes 272
  891.1 59.2 %reduce-scatter.22.cloned.1.call-done = bf16[512,64]{0,1:T(8,128)(2,1)} async-done(((bf16[512,1024]{0,1:T(8,128)(2,1)}), bf16[512,64]{0,1:T(8,128)(2,1)}) %reduce-scatter.22.cloned.1.call-update) | async-done | bytes 65552 | tf_op jit(solution)/shard_map/reduce_scatter | solution.py:212
  951.7 73.7 %reduce-scatter.26.cloned.1.call-done = bf16[2048,64]{0,1:T(8,128)(2,1)} async-done(((bf16[2048,1024]{0,1:T(8,128)(2,1)}), bf16[2048,64]{0,1:T(8,128)(2,1)}) %reduce-scatter.26.cloned.1.call-update) | async-done | bytes 262160 | tf_op jit(solution)/shard_map/reduce_scatter | solution.py:218
  1027.2 73.8 %reduce-scatter.24.cloned.1.call-done = bf16[64,2048]{1,0:T(8,128)(2,1)} async-done(((bf16[1024,2048]{1,0:T(8,128)(2,1)}), bf16[64,2048]{1,0:T(8,128)(2,1)}) %reduce-scatter.24.cloned.1.call-update) | async-done | bytes 262160 | tf_op jit(solution)/shard_map/reduce_scatter | solution.py:215
  1104.8 58.1 %all-reduce = (f32[2,512]{1,0:T(2,128)}, f32[2048]{0:T(1024)}) all-reduce(f32[2,512]{1,0:T(2,128)S(1)} %pad_maximum_fusion.3, f32[2048]{0:T(1024)S(1)} %copy-done.42), channel_id=1, replica_groups=mesh['dp'=4,'ctx'=4,'tp'=2] {'dp','ctx'}, use_global_device_ids=true, to_apply=%region_26.27 | all-reduce | flops 3072 | bytes 24576 | tf_op jit(solution)/shard_map/psum | solution.py:234
  1172.9 44.1 %reduce-scatter.30.cloned.1.call-done = bf16[64,2]{1,0:T(8,128)(2,1)} async-done(((bf16[1024,2]{1,0:T(8,128)(2,1)}), bf16[64,2]{1,0:T(8,128)(2,1)}) %reduce-scatter.30.cloned.1.call-update) | async-done | bytes 272
  1218.4 67.5 %reduce-scatter.20.cloned.1.call-done = bf16[64,3,512]{2,0,1:T(8,128)(2,1)} async-done(((bf16[1024,3,512]{2,0,1:T(8,128)(2,1)}), bf16[64,3,512]{2,0,1:T(8,128)(2,1)}) %reduce-scatter.20.cloned.1.call-update) | async-done | bytes 196624 | tf_op jit(solution)/shard_map/reduce_scatter | solution.py:209
  (242 shorter events, 175.2 us)
Async XLA Ops:
  7.2 51.0 %all-gather.11.cloned.1.call-start = ((), (), s32[]{:S(2)}) async-start(), calls=%async_computation.9 | async-start | bytes 3342336 | tf_op jit(solution)/shard_map/all_gather | solution.py:60
  7.9 93.4 %all-gather.21.cloned.1.call-start = ((), (), s32[]{:S(2)}) async-start(), calls=%async_computation.22 | async-start | bytes 5242880 | tf_op jit(solution)/shard_map/all_gather | solution.py:82
  67.8 122.6 %all-gather.13.cloned.1.call-start = ((), (), s32[]{:S(2)}) async-start(), calls=%async_computation.10 | async-start | bytes 5242880 | tf_op jit(solution)/shard_map/all_gather | solution.py:83
  70.7 165.7 %all-gather.15.cloned.1.call-start = ((), (), s32[]{:S(2)}) async-start(), calls=%async_computation.11 | async-start | bytes 1114112 | tf_op jit(solution)/shard_map/all_gather | solution.py:61
  71.3 232.5 %all-reduce.6.cloned.1.call-start = ((), (), s32[]{:S(2)}) async-start(), calls=%async_computation.12 | async-start | bytes 4194304 | tf_op jit(solution)/shard_map/psum | solution.py:107
  240.7 115.9 %all-gather.17.cloned.1.call-start = ((), (), s32[]{:S(2)}) async-start(), calls=%async_computation.13 | async-start | bytes 4456448 | tf_op jit(solution)/shard_map/all_gather | solution.py:62
  241.3 166.8 %all-gather.19.cloned.1.call-start = ((), (), s32[]{:S(2)}) async-start(), calls=%async_computation.14 | async-start | bytes 4456448 | tf_op jit(solution)/shard_map/all_gather | solution.py:63
  242.1 251.0 %all-reduce.8.cloned.1.call-start = ((), (), s32[]{:S(2)}) async-start(), calls=%async_computation.15 | async-start | bytes 4194304 | tf_op jit(solution)/shard_map/psum | solution.py:139
  262.6 238.0 %copy-start.36 = (f32[1024]{0:T(1024)}, f32[1024]{0:T(1024)S(1)}, u32[]{:S(2)}) copy-start(f32[1024]{0:T(1024)S(1)} %fusion.62) | copy-start | bytes 12292
  263.2 237.4 %copy-start.18 = (f32[1,1024]{1,0:T(1,128)}, f32[1,1024]{1,0:T(1,128)S(1)}, u32[]{:S(2)}) copy-start(f32[1,1024]{1,0:T(1,128)S(1)} %get-tuple-element.30) | copy-start | bytes 12292
  431.5 276.3 %reduce-scatter.18.cloned.1.call-start = ((), (), s32[]{:S(2)}) async-start(), calls=%async_computation.17 | async-start | bytes 5242880 | tf_op jit(solution)/shard_map/reduce_scatter | solution.py:182
  558.4 155.9 %reduce-scatter.16.cloned.1.call-start = ((), (), s32[]{:S(2)}) async-start(), calls=%async_computation.16 | async-start | bytes 5242880 | tf_op jit(solution)/shard_map/reduce_scatter | solution.py:176
  669.2 160.8 %all-reduce.10.cloned.1.call-start = ((), (), s32[]{:S(2)}) async-start(), calls=%async_computation.26 | async-start | bytes 8388608 | tf_op jit(solution)/shard_map/psum | solution.py:112
  721.6 168.1 %reduce-scatter.32.cloned.1.call-start = ((), (), s32[]{:S(2)}) async-start(), calls=%async_computation.25 | async-start | bytes 278528
  723.2 227.1 %reduce-scatter.22.cloned.1.call-start = ((), (), s32[]{:S(2)}) async-start(), calls=%async_computation.19 | async-start | bytes 1114112 | tf_op jit(solution)/shard_map/reduce_scatter | solution.py:212
  727.6 297.8 %reduce-scatter.26.cloned.1.call-start = ((), (), s32[]{:S(2)}) async-start(), calls=%async_computation.21 | async-start | bytes 4456448 | tf_op jit(solution)/shard_map/reduce_scatter | solution.py:218
  736.3 364.6 %reduce-scatter.24.cloned.1.call-start = ((), (), s32[]{:S(2)}) async-start(), calls=%async_computation.20 | async-start | bytes 4456448 | tf_op jit(solution)/shard_map/reduce_scatter | solution.py:215
  747.8 423.7 %reduce-scatter.28.cloned.1.call-start = ((), (), s32[]{:S(2)}) async-start(), calls=%async_computation.23 | async-start | bytes 278528
  838.4 378.6 %reduce-scatter.30.cloned.1.call-start = ((), (), s32[]{:S(2)}) async-start(), calls=%async_computation.24 | async-start | bytes 278528
  839.4 446.4 %reduce-scatter.20.cloned.1.call-start = ((), (), s32[]{:S(2)}) async-start(), calls=%async_computation.18 | async-start | bytes 3342336 | tf_op jit(solution)/shard_map/reduce_scatter | solution.py:209
  846.6 258.1 %copy-start.42 = (f32[2048]{0:T(1024)S(1)}, f32[2048]{0:T(1024)}, u32[]{:S(2)}) copy-start(f32[2048]{0:T(1024)} %get-tuple-element.44) | copy-start | bytes 24580
  846.6 316.3 %copy-start.29 = (f32[1024]{0:T(1024)S(1)}, f32[1024]{0:T(1024)}, u32[]{:S(2)}) copy-start(f32[1024]{0:T(1024)} %copy-done.28) | copy-start | bytes 12292
  846.6 316.3 %copy-start.39 = (f32[1024]{0:T(1024)S(1)}, f32[1024]{0:T(1024)}, u32[]{:S(2)}) copy-start(f32[1024]{0:T(1024)} %copy-done.38) | copy-start | bytes 12292
  846.6 316.3 %copy-start.40 = (f32[1,1024]{1,0:T(1,128)S(1)}, f32[1,1024]{1,0:T(1,128)}, u32[]{:S(2)}) copy-start(f32[1,1024]{1,0:T(1,128)} %get-tuple-element.29) | copy-start | bytes 12292
  (54 other events, 1557.2 us)
Sparse Core Ops, SparseCore 0:
  10.2 47.9 all-gather.10
  68.0 33.3 all-gather.20
  103.5 34.4 all-gather.12
  140.0 37.9 all-gather.14
  240.9 62.8 all-reduce.5
  306.0 50.5 all-gather.16
  359.0 49.0 all-gather.18
  431.6 61.3 all-reduce.7
  558.5 44.4 reduce-scatter.17
  669.4 44.8 reduce-scatter.15
  721.7 108.2 all-reduce.9
  834.3 55.2 reduce-scatter.31
  893.7 56.4 reduce-scatter.21
  954.0 71.4 reduce-scatter.25
  1029.6 71.2 reduce-scatter.23
  1104.9 54.3 reduce-scatter.27
  1162.6 54.3 reduce-scatter.29
  1220.6 65.1 reduce-scatter.19
where the time goes:
time: 1300 us; the launch traced here: 1290 us
  waiting for transfers between devices  657 us (51%)
  matrix products  379 us (29%)
  blocking collectives  119 us (9%)
  other arithmetic  90 us (7%)
  local copies, waits for them, and re-layouts  32.9 us (3%)
  between operations  15.2 us (1%)
    unnamed x21, waiting for transfers between devices  89.8 us
    psum x1, waiting for transfers between devices, body(): lax.psum(jnp.dot(act, w_down, preferred_element_type=jnp.float32).astype(...  81.6 us
    dot_general x1, matrix products, body(): jnp.einsum('bqhd,bkhd->bhqk', d_att_four, value_all, preferred_element_ty...  78.3 us
    reduce_scatter x1, waiting for transfers between devices, body(): lax.psum_scatter(grad_in.astype(jnp.bfloat16), ('dp', 'ctx'), scatter_dim...  73.8 us
    reduce_scatter x1, waiting for transfers between devices, body(): lax.psum_scatter(grad_down.astype(jnp.bfloat16), ('dp', 'ctx'), scatter_d...  73.7 us
    reduce_scatter x1, waiting for transfers between devices, body(): lax.psum_scatter(grad_qkv.astype(jnp.bfloat16), ('dp', 'ctx'), scatter_di...  67.5 us
    psum x1, waiting for transfers between devices, body(): lax.psum(mlp_back_part.astype(jnp.bfloat16), 'tp').astype(jnp.float32)  61.3 us
    reduce_scatter x1, waiting for transfers between devices, body(): lax.psum_scatter(grad_out.astype(jnp.bfloat16), ('dp', 'ctx'), scatter_di...  59.2 us
  transfers between devices with their start and end apart: 18, of which 14 were waited for; matrix products, arithmetic and copies ran while one was open for 30% of the time, Pallas kernels for 0%

commit v1 on v0

v1 whole, which is shorter than its diff:
```python
import functools
import math

import jax
import jax.numpy as jnp
from jax import lax
from jax.experimental import pallas as pl
from jax.experimental.pallas import tpu as pltpu
from jax.sharding import PartitionSpec as P

HD = 64
PAIR = 2 * HD
EPS = 1e-06
LOG2E = 1.4426950408889634
BF = jnp.bfloat16
F32 = jnp.float32
VMEM_LIMIT = 56 * 1024 * 1024
PAIRS_PER_CALL = 1
KEY_TILE = 512
QUERY_TILE = 256
HIDDEN_TILE = 256


def dot_nt(a, b):
    return lax.dot_general(a, b, (((1,), (1,)), ((), ())), preferred_element_type=F32)


def dot_tn(a, b):
    return lax.dot_general(a, b, (((0,), (0,)), ((), ())), preferred_element_type=F32)


def dot_nn(a, b):
    return jnp.dot(a, b, preferred_element_type=F32)


def swap_core(v):
    return lax.ppermute(v, "ctx", [(0, 1), (1, 0), (2, 3), (3, 2)])


def swap_y(v):
    return lax.ppermute(v, "ctx", [(0, 2), (2, 0), (1, 3), (3, 1)])


def gather_ctx(v):
    over = swap_y(v)
    return v, swap_core(v), over, swap_core(over)


def sum_tp(part):
    if lax.axis_size("tp") == 2:
        other = lax.ppermute(part, "tp", [(0, 1), (1, 0)])
        return part.astype(F32) + other.astype(F32)
    return lax.psum(part, "tp").astype(F32)


def gather_line(v):
    n = lax.axis_size("dp")
    z = lax.axis_index("dp")
    from_low, from_high = [], []
    up = down = v
    for _ in range(n - 1):
        up = lax.ppermute(up, "dp", [(i, i + 1) for i in range(n - 1)])
        down = lax.ppermute(down, "dp", [(i + 1, i) for i in range(n - 1)])
        from_low.append(up)
        from_high.append(down)
    held = jnp.stack(from_low[::-1] + [v] + from_high)
    return lax.dynamic_slice_in_dim(held, n - 1 - z, n, 0)


def gather_rows(shard):
    me = lax.axis_index("ctx")
    odd_core, odd_y = (me & 1) == 1, (me >> 1) == 1
    b0, b1, b2, b3 = gather_ctx(gather_line(shard))
    lo, hi = jnp.where(odd_core, b1, b0), jnp.where(odd_core, b0, b1)
    lo_far, hi_far = jnp.where(odd_core, b3, b2), jnp.where(odd_core, b2, b3)
    whole = jnp.stack(
        [
            jnp.where(odd_y, lo_far, lo),
            jnp.where(odd_y, hi_far, hi),
            jnp.where(odd_y, lo, lo_far),
            jnp.where(odd_y, hi, hi_far),
        ],
        axis=1,
    )
    return whole.reshape(-1, shard.shape[1])


def scatter_line(v):
    n = lax.axis_size("dp")
    z = lax.axis_index("dp")

    def at(i):
        return lax.dynamic_index_in_dim(v, jnp.clip(i, 0, n - 1), 0, keepdims=False)

    up, down = at(z + n - 1), at(z - n + 1)
    for step in range(1, n):
        up = lax.ppermute(up, "dp", [(i, i + 1) for i in range(n - 1)])
        down = lax.ppermute(down, "dp", [(i + 1, i) for i in range(n - 1)])
        if step < n - 1:
            up = (up.astype(F32) + at(z + n - 1 - step).astype(F32)).astype(BF)
            down = (down.astype(F32) + at(z - n + 1 + step).astype(F32)).astype(BF)
    return at(z).astype(F32) + up.astype(F32) + down.astype(F32)


def scatter_rows(v):
    n = lax.axis_size("dp")
    me = lax.axis_index("ctx")
    core, y = me & 1, me >> 1
    rows, columns = v.shape
    v = v.reshape(n, 2, 2, rows // (4 * n), columns)

    def pick(a, i, axis):
        return lax.dynamic_index_in_dim(a, i, axis, keepdims=False)

    v = (pick(v, core, 2).astype(F32) + swap_core(pick(v, 1 - core, 2)).astype(F32)).astype(BF)
    v = (pick(v, y, 1).astype(F32) + swap_y(pick(v, 1 - y, 1)).astype(F32)).astype(BF)
    return scatter_line(v)


def sum_small(v):
    n = lax.axis_size("dp")
    v = v + swap_core(v)
    v = v + swap_y(v)
    bit = 1
    while bit < n:
        v = v + lax.ppermute(v, "dp", [(i, i ^ bit) for i in range(n)])
        bit *= 2
    return v


def attend_kernel(scale, q_ref, k0, k1, k2, k3, o_ref, lse_ref):
    rows = q_ref.shape[0]
    tile = min(QUERY_TILE, rows)
    first = lax.broadcasted_iota(jnp.int32, (1, PAIR), 1) < HD

    def step(i, carry):
        at = pl.ds(pl.multiple_of(i * tile, tile), tile)
        q = q_ref[at, :]
        outs = []
        for h in range(2):
            mine = first if h == 0 else jnp.logical_not(first)
            q_h = jnp.where(mine, q, jnp.zeros_like(q))
            scores = [dot_nt(q_h, k[:, :PAIR]) for k in (k0, k1, k2, k3)]
            top = functools.reduce(
                jnp.maximum, [jnp.max(s, axis=1, keepdims=True) for s in scores]
            )
            acc = None
            for s, k in zip(scores, (k0, k1, k2, k3)):
                p = jnp.exp2((s - top) * scale).astype(BF)
                v = k[:, PAIR:]
                term = dot_nn(p, jnp.where(mine, v, jnp.ones_like(v)))
                acc = term if acc is None else acc + term
            total = pltpu.roll(acc, HD, 1)
            outs.append(acc / total)
            lse = jnp.transpose(top * scale + jnp.log2(total))
            lse_ref[0, pl.ds(h, 1), at] = lse[h * HD : h * HD + 1, :]
        o_ref[at, :] = jnp.where(first, outs[0], outs[1])
        return carry

    lax.fori_loop(0, rows // tile, step, 0)


def attend(q, blocks, call):
    rows = q.shape[0]
    width = blocks[0].shape[1] // 2
    pairs = width // PAIR
    base = call * pairs
    keys = 4 * rows
    kv_spec = pl.BlockSpec((rows, 2 * PAIR), lambda i: (0, i))
    return pl.pallas_call(
        functools.partial(attend_kernel, LOG2E / math.sqrt(HD)),
        grid=(pairs,),
        in_specs=[pl.BlockSpec((rows, PAIR), lambda i: (0, base + i))] + [kv_spec] * 4,
        out_specs=[
            pl.BlockSpec((rows, PAIR), lambda i: (0, i)),
            pl.BlockSpec((1, 8, rows), lambda i: (i, 0, 0)),
        ],
        out_shape=[
            jax.ShapeDtypeStruct((rows, width), F32),
            jax.ShapeDtypeStruct((pairs, 8, rows), F32),
        ],
        cost_estimate=pl.CostEstimate(
            flops=16 * rows * keys * width,
            bytes_accessed=rows * width * 16,
            transcendentals=rows * keys * width // HD,
        ),
        compiler_params=pltpu.CompilerParams(vmem_limit_bytes=VMEM_LIMIT),
        name="attend",
    )(q, *blocks)


def attend_back_kernel(
    scale, factor, q_ref, d_ref, o_ref, lse_ref, k0, k1, k2, k3,
    dq_ref, keep_ref, send_ref, kv, dkv, dq_turned,
):
    rows = q_ref.shape[0]
    keys = 4 * rows
    tile = min(KEY_TILE, rows)
    for place, block in enumerate((k0, k2, k1, k3)):
        kv[place * rows : (place + 1) * rows, :] = block[...]
    first = lax.broadcasted_iota(jnp.int32, (1, PAIR), 1) < HD
    d = d_ref[...]
    q = q_ref[...]
    prod = jnp.transpose(d.astype(F32) * o_ref[...])
    halves = []
    for h in range(2):
        mine = first if h == 0 else jnp.logical_not(first)
        halves.append((
            jnp.where(mine, q, jnp.zeros_like(q)),
            jnp.where(mine, d, jnp.zeros_like(d)),
            lse_ref[0, h : h + 1, :],
            jnp.sum(prod[h * HD : (h + 1) * HD, :], axis=0, keepdims=True),
        ))
    dq_turned[...] = jnp.zeros_like(dq_turned)

    def step(i, carry):
        at = pl.ds(pl.multiple_of(i * tile, tile), tile)
        k = kv[at, :PAIR]
        v = kv[at, PAIR:]
        k_turned = jnp.transpose(k)
        dk = dv = None
        for h, (q_h, d_h, lse, delta) in enumerate(halves):
            prob = jnp.exp2(dot_nt(k, q_h) * scale - lse)
            d_score = (prob * (dot_nt(v, d_h) - delta)).astype(BF)
            dv_h = dot_nn(prob.astype(BF), d_h)
            dk_h = dot_nn(d_score, q_h)
            dv = dv_h if dv is None else dv + dv_h
            dk = dk_h if dk is None else dk + dk_h
            part = slice(h * HD, (h + 1) * HD)
            dq_turned[part, :] += dot_nn(k_turned[part, :], d_score)
        dkv[at, :PAIR] = (dk * factor).astype(BF)
        dkv[at, PAIR:] = dv.astype(BF)
        return carry

    lax.fori_loop(0, keys // tile, step, 0)
    dq_ref[...] = (jnp.transpose(dq_turned[...]) * factor).astype(BF)
    keep_ref[...] = dkv[: 2 * rows, :]
    send_ref[...] = dkv[2 * rows :, :]


def attend_back(q, d_att, o, lse, blocks, call):
    rows = q.shape[0]
    width = blocks[0].shape[1] // 2
    pairs = width // PAIR
    base = call * pairs
    keys = 4 * rows
    kv_spec = pl.BlockSpec((rows, 2 * PAIR), lambda i: (0, i))
    wide = pl.BlockSpec((rows, PAIR), lambda i: (0, base + i))
    narrow = pl.BlockSpec((rows, PAIR), lambda i: (0, i))
    twice = pl.BlockSpec((2 * rows, 2 * PAIR), lambda i: (0, i))
    return pl.pallas_call(
        functools.partial(attend_back_kernel, LOG2E / math.sqrt(HD), 1.0 / math.sqrt(HD)),
        grid=(pairs,),
        in_specs=[wide, wide, narrow, pl.BlockSpec((1, 8, rows), lambda i: (i, 0, 0))]
        + [kv_spec] * 4,
        out_specs=[narrow, twice, twice],
        out_shape=[
            jax.ShapeDtypeStruct((rows, width), BF),
            jax.ShapeDtypeStruct((2 * rows, 2 * width), BF),
            jax.ShapeDtypeStruct((2 * rows, 2 * width), BF),
        ],
        scratch_shapes=[
            pltpu.VMEM((keys, 2 * PAIR), BF),
            pltpu.VMEM((keys, 2 * PAIR), BF),
            pltpu.VMEM((PAIR, rows), F32),
        ],
        cost_estimate=pl.CostEstimate(
            flops=40 * rows * keys * width,
            bytes_accessed=rows * width * 40,
            transcendentals=rows * keys * width // HD,
        ),
        compiler_params=pltpu.CompilerParams(vmem_limit_bytes=VMEM_LIMIT),
        name="attend_back",
    )(q, d_att, o, lse, *blocks)


def mlp_kernel(
    h2_ref, d_ref, in_ref, down_ref, bias_ref,
    act_ref, dpre_ref, y_ref, back_ref, bias_grad_ref, y_acc, back_acc,
):
    i = pl.program_id(0)
    w_in, w_down = in_ref[...], down_ref[...]
    pre = dot_nn(h2_ref[...], w_in) + bias_ref[...]
    d_act = dot_nn(d_ref[...], w_down)
    below = 0.5 * (1.0 + lax.erf(pre * math.sqrt(0.5)))
    act = (pre * below).astype(BF)
    slope = below + pre * (jnp.exp(-0.5 * pre * pre) * (1.0 / math.sqrt(2.0 * math.pi)))
    d_pre = (d_act * slope).astype(BF)
    act_ref[...] = act
    dpre_ref[...] = d_pre
    bias_grad_ref[...] = jnp.sum(d_pre.astype(F32), axis=0, keepdims=True)
    y = dot_nt(act, w_down)
    back = dot_nt(d_pre, w_in)

    @pl.when(i == 0)
    def _():
        y_acc[...] = y
        back_acc[...] = back

    @pl.when(i > 0)
    def _():
        y_acc[...] += y
        back_acc[...] += back

    @pl.when(i == pl.num_programs(0) - 1)
    def _():
        y_ref[...] = y_acc[...].astype(BF)
        back_ref[...] = back_acc[...].astype(BF)


def mlp(h2, d_down, w_in, w_down, bias):
    rows, width = h2.shape
    hidden = w_in.shape[1]
    tile = min(HIDDEN_TILE, hidden)
    held = pl.BlockSpec((rows, width), lambda i: (0, 0))
    weight = pl.BlockSpec((width, tile), lambda i: (0, i))
    out = pl.BlockSpec((rows, tile), lambda i: (0, i))
    line = pl.BlockSpec((1, tile), lambda i: (0, i))
    return pl.pallas_call(
        mlp_kernel,
        grid=(hidden // tile,),
        in_specs=[held, held, weight, weight, line],
        out_specs=[out, out, held, held, line],
        out_shape=[
            jax.ShapeDtypeStruct((rows, hidden), BF),
            jax.ShapeDtypeStruct((rows, hidden), BF),
            jax.ShapeDtypeStruct((rows, width), BF),
            jax.ShapeDtypeStruct((rows, width), BF),
            jax.ShapeDtypeStruct((1, hidden), F32),
        ],
        scratch_shapes=[pltpu.VMEM((rows, width), F32), pltpu.VMEM((rows, width), F32)],
        cost_estimate=pl.CostEstimate(
            flops=8 * rows * width * hidden,
            bytes_accessed=4 * width * hidden + 4 * rows * hidden + 8 * rows * width,
            transcendentals=rows * hidden,
        ),
        compiler_params=pltpu.CompilerParams(vmem_limit_bytes=VMEM_LIMIT),
        name="mlp",
    )(h2, d_down, w_in, w_down, bias)


def norm_parts(v):
    mean = jnp.mean(v, axis=-1, keepdims=True)
    centred = v - mean
    var = jnp.mean(centred * centred, axis=-1, keepdims=True)
    rstd = lax.rsqrt(var + EPS)
    return centred * rstd, rstd


def norm_back(d, unit, rstd, gain):
    d_unit = d * gain
    return rstd * (
        d_unit
        - jnp.mean(d_unit, axis=-1, keepdims=True)
        - unit * jnp.mean(d_unit * unit, axis=-1, keepdims=True)
    )


def body(
    tokens,
    lengths,
    norm_gain,
    norm_bias,
    qkv_weight,
    qv_bias,
    out_weight,
    mlp_in,
    mlp_bias,
    mlp_out,
    out_bias,
    cotangent,
):
    _, cap, width = tokens.shape
    n_ctx = lax.axis_size("ctx")
    slots = n_ctx * cap
    rows = 3 * slots // 4 // n_ctx
    spare = cap - rows
    local = qkv_weight.shape[2]
    hidden = mlp_in.shape[1]
    share = qkv_weight.shape[0]
    pairs = local // PAIR
    per_call = min(PAIRS_PER_CALL, pairs)
    calls = pairs // per_call
    me = lax.axis_index("ctx")
    shard_at = (lax.axis_index("dp") * n_ctx + me) * share

    small = jnp.concatenate([norm_gain, norm_bias, out_bias], axis=0)
    small = jnp.pad(small.T, ((0, 0), (0, PAIR - small.shape[0])))
    w_kv = jnp.stack(
        [qkv_weight[:, 1].reshape(share, pairs, PAIR), qkv_weight[:, 2].reshape(share, pairs, PAIR)],
        axis=2,
    ).reshape(share, 2 * local)
    first = gather_rows(jnp.concatenate([w_kv, small], axis=1))
    w_kv = first[:, : 2 * local]
    small = first[:, 2 * local : 2 * local + 6].T.astype(F32)
    gains, shifts, biases = small[0:2], small[2:4], small[4:6]
    second = gather_rows(jnp.concatenate([qkv_weight[:, 0], out_weight.T], axis=1))
    w_q, w_out = second[:, :local], second[:, local:]
    w_in = lax.all_gather(mlp_in, ("dp", "ctx"), axis=0, tiled=True)
    w_down = lax.all_gather(mlp_out.T, ("dp", "ctx"), axis=0, tiled=True)

    over = jnp.maximum(lengths - rows, 0)
    lack = jnp.maximum(rows - lengths, 0)
    over_at = jnp.cumsum(over) - over
    lack_at = jnp.cumsum(lack) - lack
    my_length = lengths[me]
    row = lax.iota(jnp.int32, rows)
    own = row < my_length
    need = jnp.where(own, -1, lack_at[me] + row - my_length)
    column = lax.iota(jnp.int32, n_ctx * spare)
    owner = (column // spare) ^ me
    source = jnp.where(column % spare < over[owner], over_at[owner] + column % spare, -2)
    pick = (need[:, None] == source[None, :]).astype(BF)

    def take(v):
        blocks = jnp.concatenate(gather_ctx(v[rows:]), axis=0)
        return jnp.where(own[:, None], v[:rows], dot_nn(pick, blocks).astype(BF))

    def give(v):
        blocks = dot_tn(pick, v).astype(BF)
        near, far = blocks[spare : 2 * spare], blocks[3 * spare :]
        got = swap_core(jnp.concatenate([near, far], axis=0))
        back = swap_y(blocks[2 * spare : 3 * spare] + got[spare:])
        kept = jnp.where(own[:, None], v, jnp.zeros_like(v))
        return jnp.concatenate([kept, got[:spare] + back], axis=0)[None]

    x = take(tokens[0]).astype(F32)
    d_down = take(cotangent[0])

    unit_one, rstd_one = norm_parts(x)
    h1 = (unit_one * gains[0] + shifts[0]).astype(BF)
    kv_bias = jnp.stack(
        [jnp.zeros((pairs, PAIR), F32), qv_bias[1].reshape(pairs, PAIR)], axis=1
    ).reshape(2 * local)
    kv_blocks = []
    for call in range(calls):
        at = slice(call * per_call * 2 * PAIR, (call + 1) * per_call * 2 * PAIR)
        kv = (dot_nn(h1, w_kv[:, at]) + kv_bias[at]).astype(BF)
        kv_blocks.append(gather_ctx(kv))
    query = (dot_nn(h1, w_q) + qv_bias[0]).astype(BF)
    attn, lse = [], []
    for call in range(calls):
        o, l = attend(query, kv_blocks[call], call)
        attn.append(o)
        lse.append(l)
    attended = jnp.concatenate([o.astype(BF) for o in attn], axis=1)
    x_one = x + (sum_tp(dot_nt(attended, w_out).astype(BF)) + biases[0])
    unit_two, rstd_two = norm_parts(x_one)
    h2 = (unit_two * gains[1] + shifts[1]).astype(BF)
    act, d_pre, y_part, back_part, mlp_bias_grad = mlp(h2, d_down, w_in, w_down, mlp_bias[None])
    d_h2 = sum_tp(back_part)
    grad_in = lax.psum_scatter(
        dot_tn(h2, d_pre).astype(BF), ("dp", "ctx"), scatter_dimension=0, tiled=True
    ).astype(F32)
    grad_down = (
        lax.psum_scatter(
            dot_tn(d_down, act).astype(BF), ("dp", "ctx"), scatter_dimension=0, tiled=True
        )
        .astype(F32)
        .T
    )

    d_x_one = d_down.astype(F32) + norm_back(d_h2, unit_two, rstd_two, gains[1])
    d_branch = d_x_one.astype(BF)
    d_att = dot_nn(d_branch, w_out).astype(BF)
    result = give((x_one + (sum_tp(y_part) + biases[1])).astype(BF))

    d_query, d_kv = [], []
    for call in range(calls):
        dq, keep, send = attend_back(query, d_att, attn[call], lse[call], kv_blocks[call], call)
        got = swap_core(send)
        far = swap_y((keep[rows:].astype(F32) + got[rows:].astype(F32)).astype(BF))
        d_kv.append(
            (keep[:rows].astype(F32) + got[:rows].astype(F32) + far.astype(F32)).astype(BF)
        )
        d_query.append(dq)
    d_query = jnp.concatenate(d_query, axis=1)
    d_kv = jnp.concatenate(d_kv, axis=1)

    attn_back = dot_nt(d_query, w_q) + dot_nt(d_kv, w_kv)
    attn_back = attn_back.astype(BF)
    d_h1 = sum_tp(attn_back)
    grad_tokens = give((d_x_one + norm_back(d_h1, unit_one, rstd_one, gains[0])).astype(BF))

    grad_attn = jnp.concatenate(
        [dot_tn(h1, d_query), dot_tn(h1, d_kv), dot_tn(d_branch, attended)], axis=1
    ).astype(BF)
    grad_attn = scatter_rows(grad_attn)
    grad_q = grad_attn[:, :local]
    grad_kv = grad_attn[:, local : 3 * local].reshape(share, pairs, 2, PAIR)
    grad_qkv = jnp.stack(
        [grad_q, grad_kv[:, :, 0].reshape(share, local), grad_kv[:, :, 1].reshape(share, local)],
        axis=1,
    )
    grad_out = grad_attn[:, 3 * local :].T

    q_sum = jnp.sum(d_query.astype(F32), axis=0)
    v_sum = jnp.sum(d_kv.astype(F32), axis=0).reshape(pairs, 2, PAIR)[:, 1].reshape(local)
    sums = jnp.concatenate([
        jnp.sum(d_h1 * unit_one, axis=0),
        jnp.sum(d_h2 * unit_two, axis=0),
        jnp.sum(d_h1, axis=0),
        jnp.sum(d_h2, axis=0),
        jnp.sum(d_branch.astype(F32), axis=0),
        jnp.sum(d_down.astype(F32), axis=0),
        q_sum,
        v_sum,
        mlp_bias_grad[0],
    ])
    sums = sum_small(sums.reshape(-1, PAIR)).reshape(-1)
    wide = lax.dynamic_slice(sums[: 6 * width].reshape(6, width), (0, shard_at), (6, share))
    qv_grad = sums[6 * width : 6 * width + 2 * local].reshape(2, local)
    mlp_bias_sum = sums[6 * width + 2 * local :]
    return (
        result,
        grad_tokens,
        wide[0:2],
        wide[2:4],
        grad_qkv,
        qv_grad,
        grad_out,
        grad_in,
        mlp_bias_sum,
        grad_down,
        wide[4:6],
    )


def solution(mesh):
    in_specs = (
        P("dp", "ctx", None),
        P(),
        P(None, ("dp", "ctx")),
        P(None, ("dp", "ctx")),
        P(("dp", "ctx"), None, "tp"),
        P(None, "tp"),
        P("tp", ("dp", "ctx")),
        P(("dp", "ctx"), "tp"),
        P("tp"),
        P("tp", ("dp", "ctx")),
        P(None, ("dp", "ctx")),
        P("dp", "ctx", None),
    )
    out_specs = (
        P("dp", "ctx", None),
        P("dp", "ctx", None),
        P(None, ("dp", "ctx")),
        P(None, ("dp", "ctx")),
        P(("dp", "ctx"), None, "tp"),
        P(None, "tp"),
        P("tp", ("dp", "ctx")),
        P(("dp", "ctx"), "tp"),
        P("tp"),
        P("tp", ("dp", "ctx")),
        P(None, ("dp", "ctx")),
    )
    return jax.shard_map(body, mesh=mesh, in_specs=in_specs, out_specs=out_specs, check_vma=False)
```

time: 1300 us -> 568 us (0.44)
  waiting for transfers between devices: 657 us -> 221 us
  matrix products: 379 us -> 38.8 us
  Pallas kernels: 0 us -> 130 us
  blocking collectives: 119 us -> 0 us
  starting transfers between devices: 1.99 us -> 79.9 us
  other arithmetic: 90 us -> 58 us
  local copies, waits for them, and re-layouts: 32.9 us -> 19.6 us
    dot_general x18, matrix products: 379 us -> 38.8 us  [the longest x7 23.8 us: dot_tn(): lax.dot_general(a, b, (((0,), (0,)), ((), ())), preferred_element_type=F32)]
    reduce_scatter x6 -> x2, waiting for transfers between devices: 281 us -> 0.02 us  [the longest x1 0.02 us: body(): lax.psum_scatter(dot_tn(d_down, act).astype(BF), ('dp', 'ctx'), scatter_d...]
    ppermute x0 -> x64, waiting for transfers between devices: none -> 221 us  [the longest x16 99.8 us: swap_y(): return lax.ppermute(v, 'ctx', [(0, 2), (2, 0), (1, 3), (3, 1)])]
    psum x3 -> x0, waiting for transfers between devices: 183 us -> none  [the longest x1 81.6 us: body(): lax.psum(jnp.dot(act, w_down, preferred_element_type=jnp.float32).astype(...]
    pallas_call x0 -> x9, Pallas kernels: none -> 130 us  [the longest x4 65.3 us: attend_back(): pl.pallas_call(functools.partial(attend_back_kernel, LOG2E / math.sqrt(HD...]
    all_gather x6 -> x2, waiting for transfers between devices: 103 us -> 0.01 us  [the longest x1 0.01 us: body(): w_in = lax.all_gather(mlp_in, ('dp', 'ctx'), axis=0, tiled=True)]
    unnamed x21 -> x4, waiting for transfers between devices: 89.8 us -> 0.73 us
    ppermute x0 -> x64, starting transfers between devices: none -> 79.7 us  [the longest x6 28.2 us: gather_line(): up = lax.ppermute(up, 'dp', [(i, i + 1) for i in range(n - 1)])]
  transfers between devices with their start and end apart: 18 -> 68, of which waited for: 14 -> 28; matrix products, arithmetic and copies ran while one was open for 30% -> 18% of each run, Pallas kernels for 0% -> 18%
where the time goes in v1:
time: 568 us; the launch traced here: 564 us
  waiting for transfers between devices  221 us (39%)
  Pallas kernels  130 us (23%)
  starting transfers between devices  79.9 us (14%)
  other arithmetic  58 us (10%)
  matrix products  38.8 us (7%)
  local copies, waits for them, and re-layouts  19.6 us (3%)
  between operations  15.8 us (3%)
    ppermute x16, waiting for transfers between devices, swap_y(): return lax.ppermute(v, 'ctx', [(0, 2), (2, 0), (1, 3), (3, 1)])  99.8 us
    ppermute x4, waiting for transfers between devices, sum_tp(): other = lax.ppermute(part, 'tp', [(0, 1), (1, 0)])  84.2 us
    pallas_call x4, Pallas kernels, attend_back(): pl.pallas_call(functools.partial(attend_back_kernel, LOG2E / math.sqrt(HD...  65.3 us
    pallas_call x4, Pallas kernels, attend(): pl.pallas_call(functools.partial(attend_kernel, LOG2E / math.sqrt(HD)), g...  38.6 us
    ppermute x6, starting transfers between devices, gather_line(): up = lax.ppermute(up, 'dp', [(i, i + 1) for i in range(n - 1)])  28.2 us
    pallas_call x1, Pallas kernels, mlp(): pl.pallas_call(mlp_kernel, grid=(hidden // tile,), in_specs=[held, held,...  26.6 us
    dot_general x7, matrix products, dot_tn(): lax.dot_general(a, b, (((0,), (0,)), ((), ())), preferred_element_type=F32)  23.8 us
    ppermute x16, starting transfers between devices, swap_y(): return lax.ppermute(v, 'ctx', [(0, 2), (2, 0), (1, 3), (3, 1)])  22.2 us
  transfers between devices with their start and end apart: 68, of which 28 were waited for; matrix products, arithmetic and copies ran while one was open for 18% of the time, Pallas kernels for 18%

profile of v1, /device:TPU:0, one launch (start us, length us, event | category | flops | bytes accessed | tf_op | source)
XLA Modules:
  0.0 563.7 jit_solution(118999682512122615)
XLA Ops:
  68.6 6.0 %collective-permute-done.8 = bf16[64,1152]{1,0:T(8,128)(2,1)S(1)} collective-permute-done((bf16[64,1152]{1,0:T(8,128)(2,1)S(1)}, bf16[64,1152]{1,0:T(8,128)(2,1)S(1)}, u32[]{:S(2)}, u32[]{:S(2)}) %collective-permute-start.8) | collective-permute-done | bytes 147488 | tf_op jit(solution)/shard_map/ppermute | solution.py:63
  83.9 22.4 %collective-permute-done.18 = bf16[4,64,1024]{2,1,0:T(8,128)(2,1)S(1)} collective-permute-done((bf16[4,64,1024]{2,1,0:T(8,128)(2,1)S(1)}, bf16[4,64,1024]{2,1,0:T(8,128)(2,1)S(1)}, u32[]{:S(2)}, u32[]{:S(2)}) %collective-permute-start.18) | collective-permute-done | bytes 524320 | tf_op jit(solution)/shard_map/ppermute | solution.py:41
  118.2 8.1 %collective-permute-done.22.k2 = bf16[768,256]{1,0:T(8,128)(2,1)S(1)} collective-permute-done((bf16[768,256]{1,0:T(8,128)(2,1)S(1)}, bf16[768,256]{1,0:T(8,128)(2,1)S(1)}, u32[]{:S(2)}, u32[]{:S(2)}) %collective-permute-start.22) | collective-permute-done | bytes 393248 | tf_op jit(solution)/shard_map/ppermute | solution.py:41
  137.5 9.7 %attend.4 = (f32[768,128]{1,0:T(8,128)}, f32[1,8,768]{2,1,0:T(8,128)}) custom-call(bf16[768,512]{1,0:T(8,128)(2,1)} %add_convert_fusion.3.q_ref, bf16[768,256]{1,0:T(8,128)(2,1)} %copy-done.56, bf16[768,256]{1,0:T(8,128)(2,1)} %copy-done.58, bf16[768,256]{1,0:T(8,128)(2,1)} %copy-done.57, bf16[768,256]{1,0:T(8,128)(2,1)} %copy-done.61), custom_call_target="tpu_custom_call" | custom-call | flops 4831838208 | bytes 1572864 | tf_op jit(solution)/shard_map/attend/pallas_call | solution.py:170
  151.9 9.5 %attend.5 = (f32[768,128]{1,0:T(8,128)}, f32[1,8,768]{2,1,0:T(8,128)}) custom-call(bf16[768,512]{1,0:T(8,128)(2,1)} %add_convert_fusion.3.q_ref, bf16[768,256]{1,0:T(8,128)(2,1)} %copy-done.53, bf16[768,256]{1,0:T(8,128)(2,1)} %collective-permute-done.24.k1, bf16[768,256]{1,0:T(8,128)(2,1)} %copy-done.54, bf16[768,256]{1,0:T(8,128)(2,1)} %collective-permute-done.26.k3), custom_call_target="tpu_custom_call" | custom-call | flops 4831838208 | bytes 1572864 | tf_op jit(solution)/shard_map/attend/pallas_call | solution.py:170
  162.5 9.6 %attend.6 = (f32[768,128]{1,0:T(8,128)}, f32[1,8,768]{2,1,0:T(8,128)}) custom-call(bf16[768,512]{1,0:T(8,128)(2,1)} %add_convert_fusion.3.q_ref, bf16[768,256]{1,0:T(8,128)(2,1)} %copy-done.52, bf16[768,256]{1,0:T(8,128)(2,1)} %collective-permute-done.27.k1, bf16[768,256]{1,0:T(8,128)(2,1)} %copy-done.59, bf16[768,256]{1,0:T(8,128)(2,1)} %collective-permute-done.29.k3), custom_call_target="tpu_custom_call" | custom-call | flops 4831838208 | bytes 1572864 | tf_op jit(solution)/shard_map/attend/pallas_call | solution.py:170
  174.6 9.8 %attend.7 = (f32[768,128]{1,0:T(8,128)}, f32[1,8,768]{2,1,0:T(8,128)}) custom-call(bf16[768,512]{1,0:T(8,128)(2,1)} %add_convert_fusion.3.q_ref, bf16[768,256]{1,0:T(8,128)(2,1)} %copy-done.51, bf16[768,256]{1,0:T(8,128)(2,1)} %copy-done.60, bf16[768,256]{1,0:T(8,128)(2,1)} %copy-done.55, bf16[768,256]{1,0:T(8,128)(2,1)} %copy-done.62), custom_call_target="tpu_custom_call" | custom-call | flops 4831838208 | bytes 1572864 | tf_op jit(solution)/shard_map/attend/pallas_call | solution.py:170
  193.6 29.3 %collective-permute-done.33 = bf16[768,1024]{1,0:T(8,128)(2,1)S(1)} collective-permute-done((bf16[768,1024]{1,0:T(8,128)(2,1)S(1)}, bf16[768,1024]{1,0:T(8,128)(2,1)S(1)}, u32[]{:S(2)}, u32[]{:S(2)}) %collective-permute-start.33) | collective-permute-done | bytes 1572896 | tf_op jit(solution)/shard_map/ppermute | solution.py:51
  225.9 26.6 %mlp.1 = (bf16[768,2048]{1,0:T(8,128)(2,1)}, bf16[768,2048]{1,0:T(8,128)(2,1)}, bf16[768,1024]{1,0:T(8,128)(2,1)}, bf16[768,1024]{1,0:T(8,128)(2,1)}, f32[1,2048]{1,0:T(1,128)}) custom-call(bf16[768,1024]{1,0:T(8,128)(2,1)} %add_convert_fusion.2.h2_ref, bf16[768,1024]{1,0:T(8,128)(2,1)} %bitcast_select_fusion.d_ref, ...), custom_call_target="tpu_custom_call" | custom-call | flops 12884901888 | bytes 20971520 | tf_op jit(solution)/shard_map/mlp/pallas_call | solution.py:319
  252.5 7.0 %convolution_convert_fusion.1 = bf16[1024,2048]{1,0:T(8,128)(2,1)} fusion(bf16[768,1024]{1,0:T(8,128)(2,1)S(1)} %copy-done.15, bf16[768,2048]{1,0:T(8,128)(2,1)} %get-tuple-element.59), kind=kOutput, calls=%fused_computation.17 | convolution fusion | flops 3223322624 | bytes 8912896 | tf_op jit(solution)/shard_map/dot_general | solution.py:29
  261.7 8.1 %convolution_convert_fusion = bf16[1024,2048]{1,0:T(8,128)(2,1)} fusion(bf16[768,1024]{1,0:T(8,128)(2,1)} %bitcast_select_fusion.d_ref, bf16[768,2048]{1,0:T(8,128)(2,1)} %get-tuple-element.60), kind=kOutput, calls=%fused_computation.16 | convolution fusion | flops 3223322624 | bytes 8912896 | tf_op jit(solution)/shard_map/dot_general | solution.py:29
  269.8 27.5 %collective-permute-done.40 = bf16[768,1024]{1,0:T(8,128)(2,1)} collective-permute-done((bf16[768,1024]{1,0:T(8,128)(2,1)}, bf16[768,1024]{1,0:T(8,128)(2,1)}, u32[]{:S(2)}, u32[]{:S(2)}) %collective-permute-start.40) | collective-permute-done | bytes 1572896 | tf_op jit(solution)/shard_map/ppermute | solution.py:51
  308.8 16.3 %attend_back.4 = (bf16[768,128]{1,0:T(8,128)(2,1)}, bf16[1536,256]{1,0:T(8,128)(2,1)}, bf16[1536,256]{1,0:T(8,128)(2,1)}) custom-call(bf16[768,512]{1,0:T(8,128)(2,1)} %add_convert_fusion.3.q_ref, bf16[768,512]{1,0:T(8,128)(2,1)} %convolution_convert_fusion.6.d_ref, f32[768,128]{1,0:T(8,128)} %get-tuple-element.36.o_ref, ...), custom_call_target="tpu_custom_call" | custom-call | flops 12079595520 | bytes 3932160 | tf_op jit(solution)/shard_map/attend_back/pallas_call | solution.py:251
  326.1 16.2 %attend_back.5 = (bf16[768,128]{1,0:T(8,128)(2,1)}, bf16[1536,256]{1,0:T(8,128)(2,1)}, bf16[1536,256]{1,0:T(8,128)(2,1)}) custom-call(bf16[768,512]{1,0:T(8,128)(2,1)} %add_convert_fusion.3.q_ref, bf16[768,512]{1,0:T(8,128)(2,1)} %convolution_convert_fusion.6.d_ref, f32[768,128]{1,0:T(8,128)} %get-tuple-element.37.o_ref, ...), custom_call_target="tpu_custom_call" | custom-call | flops 12079595520 | bytes 3932160 | tf_op jit(solution)/shard_map/attend_back/pallas_call | solution.py:251
  342.8 16.4 %attend_back.6 = (bf16[768,128]{1,0:T(8,128)(2,1)}, bf16[1536,256]{1,0:T(8,128)(2,1)}, bf16[1536,256]{1,0:T(8,128)(2,1)}) custom-call(bf16[768,512]{1,0:T(8,128)(2,1)} %add_convert_fusion.3.q_ref, bf16[768,512]{1,0:T(8,128)(2,1)} %convolution_convert_fusion.6.d_ref, f32[768,128]{1,0:T(8,128)} %get-tuple-element.38.o_ref, ...), custom_call_target="tpu_custom_call" | custom-call | flops 12079595520 | bytes 3932160 | tf_op jit(solution)/shard_map/attend_back/pallas_call | solution.py:251
  359.2 16.5 %attend_back.7 = (bf16[768,128]{1,0:T(8,128)(2,1)}, bf16[1536,256]{1,0:T(8,128)(2,1)}, bf16[1536,256]{1,0:T(8,128)(2,1)}) custom-call(bf16[768,512]{1,0:T(8,128)(2,1)} %add_convert_fusion.3.q_ref, bf16[768,512]{1,0:T(8,128)(2,1)} %convolution_convert_fusion.6.d_ref, f32[768,128]{1,0:T(8,128)} %get-tuple-element.39.o_ref, ...), custom_call_target="tpu_custom_call" | custom-call | flops 12079595520 | bytes 3932160 | tf_op jit(solution)/shard_map/attend_back/pallas_call | solution.py:251
  385.5 5.4 collective-permute-done.42
  392.0 10.1 %collective-permute-done.44 = bf16[768,256]{1,0:T(8,128)(2,1)S(1)} collective-permute-done((bf16[768,256]{1,0:T(8,128)(2,1)S(1)}, bf16[768,256]{1,0:T(8,128)(2,1)S(1)}, u32[]{:S(2)}, u32[]{:S(2)}) %collective-permute-start.44) | collective-permute-done | bytes 393248 | tf_op jit(solution)/shard_map/ppermute | solution.py:41
  403.2 7.2 %collective-permute-done.46 = bf16[768,256]{1,0:T(8,128)(2,1)S(1)} collective-permute-done((bf16[768,256]{1,0:T(8,128)(2,1)S(1)}, bf16[768,256]{1,0:T(8,128)(2,1)S(1)}, u32[]{:S(2)}, u32[]{:S(2)}) %collective-permute-start.46) | collective-permute-done | bytes 393248 | tf_op jit(solution)/shard_map/ppermute | solution.py:41
  411.7 6.5 %collective-permute-done.48 = bf16[768,256]{1,0:T(8,128)(2,1)S(1)} collective-permute-done((bf16[768,256]{1,0:T(8,128)(2,1)S(1)}, bf16[768,256]{1,0:T(8,128)(2,1)S(1)}, u32[]{:S(2)}, u32[]{:S(2)}) %collective-permute-start.48) | collective-permute-done | bytes 393248 | tf_op jit(solution)/shard_map/ppermute | solution.py:41
  429.6 27.4 %collective-permute-done.49 = bf16[768,1024]{1,0:T(8,128)(2,1)S(1)} collective-permute-done((bf16[768,1024]{1,0:T(8,128)(2,1)S(1)}, bf16[768,1024]{1,0:T(8,128)(2,1)S(1)}, u32[]{:S(2)}, u32[]{:S(2)}) %collective-permute-start.49) | collective-permute-done | bytes 1572896 | tf_op jit(solution)/shard_map/ppermute | solution.py:51
  491.8 18.6 %collective-permute-done.57 = bf16[4,64,2048]{2,1,0:T(8,128)(2,1)S(1)} collective-permute-done((bf16[4,64,2048]{2,1,0:T(8,128)(2,1)S(1)}, bf16[4,64,2048]{2,1,0:T(8,128)(2,1)S(1)}, u32[]{:S(2)}, u32[]{:S(2)}) %collective-permute-start.57) | collective-permute-done | bytes 1048608 | tf_op jit(solution)/shard_map/ppermute | solution.py:41
  514.2 7.4 %collective-permute-done.51 = bf16[256,1024]{1,0:T(8,128)(2,1)S(1)} collective-permute-done((bf16[256,1024]{1,0:T(8,128)(2,1)S(1)}, bf16[256,1024]{1,0:T(8,128)(2,1)S(1)}, u32[]{:S(2)}, u32[]{:S(2)}) %collective-permute-start.51) | collective-permute-done | bytes 524320 | tf_op jit(solution)/shard_map/ppermute | solution.py:41
  521.7 7.5 %collective-permute-done.39 = bf16[256,1024]{1,0:T(8,128)(2,1)S(1)} collective-permute-done((bf16[256,1024]{1,0:T(8,128)(2,1)S(1)}, bf16[256,1024]{1,0:T(8,128)(2,1)S(1)}, u32[]{:S(2)}, u32[]{:S(2)}) %collective-permute-start.39) | collective-permute-done | bytes 524320 | tf_op jit(solution)/shard_map/ppermute | solution.py:41
  (403 shorter events, 219.1 us)
Async XLA Ops:
  7.2 218.7 %all-gather.3.cloned.1.call-start = ((), (), s32[]{:S(2)}) async-start(), calls=%async_computation.2 | async-start | bytes 4456448 | tf_op jit(solution)/shard_map/all_gather | solution.py:399
  7.9 218.0 %all-gather.5.cloned.1.call-start = ((), (), s32[]{:S(2)}) async-start(), calls=%async_computation.3 | async-start | bytes 4456448 | tf_op jit(solution)/shard_map/all_gather | solution.py:400
  10.2 32.5 %collective-permute-start.3 = (bf16[64,1152]{1,0:T(8,128)(2,1)S(1)}, bf16[64,1152]{1,0:T(8,128)(2,1)S(1)}, u32[]{:S(2)}, u32[]{:S(2)}) collective-permute-start(bf16[64,1152]{1,0:T(8,128)(2,1)S(1)} %fusion.97), channel_id=1, source_target_pairs={{0,8},{8,16},{16,24},{1,9},{9,17},{17,25},{2,10},{10,18},{18,26},{... | collective-permute-start | bytes 442376 | tf_op jit(solution)/shard_map/ppermute | solution.py:62
  15.2 27.6 %collective-permute-start.6 = (bf16[64,1152]{1,0:T(8,128)(2,1)S(1)}, bf16[64,1152]{1,0:T(8,128)(2,1)S(1)}, u32[]{:S(2)}, u32[]{:S(2)}) collective-permute-start(bf16[64,1152]{1,0:T(8,128)(2,1)S(1)} %fusion.97), channel_id=1, source_target_pairs={{8,0},{16,8},{24,16},{9,1},{17,9},{25,17},{10,2},{18,10},{26,18},{... | collective-permute-start | bytes 442376 | tf_op jit(solution)/shard_map/ppermute | solution.py:63
  24.3 52.6 %collective-permute-start.1 = (bf16[256,1024]{1,0:T(8,128)(2,1)S(1)}, bf16[256,1024]{1,0:T(8,128)(2,1)S(1)}, u32[]{:S(2)}, u32[]{:S(2)}) collective-permute-start(bf16[256,1024]{1,0:T(8,128)(2,1)S(1)} %slice_bitcast_fusion.1), channel_id=1, source_target_pairs={{0,4},{4,0},{2,6},{6,2},{1,5},{5,1},{3,7},{7,3},{8,12},{12,8},{10,... | collective-permute-start | bytes 1572872 | tf_op jit(solution)/shard_map/ppermute | solution.py:41
  25.9 511.1 %reduce-scatter.3.cloned.1.call-start = ((), (), s32[]{:S(2)}) async-start(), calls=%async_computation.4 | async-start | bytes 4456448 | tf_op jit(solution)/shard_map/reduce_scatter | solution.py:452
  42.7 40.6 %collective-permute-start = (bf16[256,1024]{1,0:T(8,128)(2,1)S(1)}, bf16[256,1024]{1,0:T(8,128)(2,1)S(1)}, u32[]{:S(2)}, u32[]{:S(2)}) collective-permute-start(bf16[256,1024]{1,0:T(8,128)(2,1)S(1)} %slice_bitcast_fusion.1), channel_id=1, source_target_pairs={{0,2},{2,0},{4,6},{6,4},{1,3},{3,1},{5,7},{7,5},{8,10},{10,8},{12,... | collective-permute-start | bytes 1572872 | tf_op jit(solution)/shard_map/ppermute | solution.py:37
  54.0 133.9 %collective-permute-start.35 = (bf16[256,1024]{1,0:T(8,128)(2,1)S(1)}, bf16[256,1024]{1,0:T(8,128)(2,1)S(1)}, u32[]{:S(2)}, u32[]{:S(2)}) collective-permute-start(bf16[256,1024]{1,0:T(8,128)(2,1)S(1)} %slice_bitcast_fusion), channel_id=1, source_target_pairs={{0,4},{4,0},{2,6},{6,2},{1,5},{5,1},{3,7},{7,3},{8,12},{12,8},{10,... | collective-permute-start | bytes 1572872 | tf_op jit(solution)/shard_map/ppermute | solution.py:41
  74.7 31.7 %collective-permute-start.9 = (bf16[4,64,1152]{2,1,0:T(8,128)(2,1)S(1)}, bf16[4,64,1152]{2,1,0:T(8,128)(2,1)S(1)}, u32[]{:S(2)}, u32[]{:S(2)}) collective-permute-start(bf16[4,64,1152]{2,1,0:T(8,128)(2,1)S(1)} %constant_dynamic-slice_fusion.4), channel_id=1, source_target_pairs={{0,4},{4,0},{2,6},{6,2},{1,5},{5,1},{3,7},{7,3},{8,12},{12,8},{10,... | collective-permute-start | bytes 1769480 | tf_op jit(solution)/shard_map/ppermute | solution.py:41
  76.5 29.9 %collective-permute-start.18 = (bf16[4,64,1024]{2,1,0:T(8,128)(2,1)S(1)}, bf16[4,64,1024]{2,1,0:T(8,128)(2,1)S(1)}, u32[]{:S(2)}, u32[]{:S(2)}) collective-permute-start(bf16[4,64,1024]{2,1,0:T(8,128)(2,1)S(1)} %constant_dynamic-slice_fusion.3), channel_id=1, source_target_pairs={{0,4},{4,0},{2,6},{6,2},{1,5},{5,1},{3,7},{7,3},{8,12},{12,8},{10,... | collective-permute-start | bytes 1572872 | tf_op jit(solution)/shard_map/ppermute | solution.py:41
  76.8 30.0 %collective-permute-start.2 = (bf16[256,1024]{1,0:T(8,128)(2,1)S(1)}, bf16[256,1024]{1,0:T(8,128)(2,1)S(1)}, u32[]{:S(2)}, u32[]{:S(2)}) collective-permute-start(bf16[256,1024]{1,0:T(8,128)(2,1)S(1)} %collective-permute-done.1), channel_id=1, source_target_pairs={{0,2},{2,0},{4,6},{6,4},{1,3},{3,1},{5,7},{7,5},{8,10},{10,8},{12,... | collective-permute-start | bytes 1572872 | tf_op jit(solution)/shard_map/ppermute | solution.py:37
  117.5 30.7 %collective-permute-start.24 = (bf16[768,256]{1,0:T(8,128)(2,1)S(1)}, bf16[768,256]{1,0:T(8,128)(2,1)}, u32[]{:S(2)}, u32[]{:S(2)}) collective-permute-start(bf16[768,256]{1,0:T(8,128)(2,1)S(1)} %fusion.72.k0), channel_id=1, source_target_pairs={{0,2},{2,0},{4,6},{6,4},{1,3},{3,1},{5,7},{7,5},{8,10},{10,8},{12,... | collective-permute-start | bytes 1179656 | tf_op jit(solution)/shard_map/ppermute | solution.py:37
  186.5 36.4 %collective-permute-start.33 = (bf16[768,1024]{1,0:T(8,128)(2,1)S(1)}, bf16[768,1024]{1,0:T(8,128)(2,1)S(1)}, u32[]{:S(2)}, u32[]{:S(2)}) collective-permute-start(bf16[768,1024]{1,0:T(8,128)(2,1)S(1)} %convolution_convert_fusion.3), channel_id=1, source_target_pairs={{0,1},{1,0},{2,3},{3,2},{4,5},{5,4},{6,7},{7,6},{8,9},{9,8},{10,11... | collective-permute-start | bytes 4718600 | tf_op jit(solution)/shard_map/ppermute | solution.py:51
  259.5 287.8 %reduce-scatter.5.cloned.1.call-start = ((), (), s32[]{:S(2)}) async-start(), calls=%async_computation.5 | async-start | bytes 4456448 | tf_op jit(solution)/shard_map/reduce_scatter | solution.py:456
  259.6 37.7 %collective-permute-start.40 = (bf16[768,1024]{1,0:T(8,128)(2,1)}, bf16[768,1024]{1,0:T(8,128)(2,1)}, u32[]{:S(2)}, u32[]{:S(2)}) collective-permute-start(bf16[768,1024]{1,0:T(8,128)(2,1)} %get-tuple-element.41), channel_id=1, source_target_pairs={{0,1},{1,0},{2,3},{3,2},{4,5},{5,4},{6,7},{7,6},{8,9},{9,8},{10,11... | collective-permute-start | bytes 4718600 | tf_op jit(solution)/shard_map/ppermute | solution.py:51
  260.9 198.3 %collective-permute-start.37 = (bf16[768,1024]{1,0:T(8,128)(2,1)}, bf16[768,1024]{1,0:T(8,128)(2,1)}, u32[]{:S(2)}, u32[]{:S(2)}) collective-permute-start(bf16[768,1024]{1,0:T(8,128)(2,1)} %get-tuple-element.40), channel_id=1, source_target_pairs={{0,1},{1,0},{2,3},{3,2},{4,5},{5,4},{6,7},{7,6},{8,9},{9,8},{10,11... | collective-permute-start | bytes 4718600 | tf_op jit(solution)/shard_map/ppermute | solution.py:51
  326.1 51.5 %collective-permute-start.41 = (bf16[1536,256]{1,0:T(8,128)(2,1)}, bf16[1536,256]{1,0:T(8,128)(2,1)}, u32[]{:S(2)}, u32[]{:S(2)}) collective-permute-start(bf16[1536,256]{1,0:T(8,128)(2,1)} %get-tuple-element.51), channel_id=1, source_target_pairs={{0,2},{2,0},{4,6},{6,4},{1,3},{3,1},{5,7},{7,5},{8,10},{10,8},{12,... | collective-permute-start | bytes 2359304 | tf_op jit(solution)/shard_map/ppermute | solution.py:37
  342.3 38.3 %collective-permute-start.43 = (bf16[1536,256]{1,0:T(8,128)(2,1)}, bf16[1536,256]{1,0:T(8,128)(2,1)}, u32[]{:S(2)}, u32[]{:S(2)}) collective-permute-start(bf16[1536,256]{1,0:T(8,128)(2,1)} %get-tuple-element.53), channel_id=1, source_target_pairs={{0,2},{2,0},{4,6},{6,4},{1,3},{3,1},{5,7},{7,5},{8,10},{10,8},{12,... | collective-permute-start | bytes 2359304 | tf_op jit(solution)/shard_map/ppermute | solution.py:37
  383.2 27.3 %collective-permute-start.46 = (bf16[768,256]{1,0:T(8,128)(2,1)S(1)}, bf16[768,256]{1,0:T(8,128)(2,1)S(1)}, u32[]{:S(2)}, u32[]{:S(2)}) collective-permute-start(bf16[768,256]{1,0:T(8,128)(2,1)S(1)} %add_convert_fusion.7), channel_id=1, source_target_pairs={{0,4},{4,0},{2,6},{6,2},{1,5},{5,1},{3,7},{7,3},{8,12},{12,8},{10,... | collective-permute-start | bytes 1179656 | tf_op jit(solution)/shard_map/ppermute | solution.py:41
  385.2 33.0 %collective-permute-start.48 = (bf16[768,256]{1,0:T(8,128)(2,1)S(1)}, bf16[768,256]{1,0:T(8,128)(2,1)S(1)}, u32[]{:S(2)}, u32[]{:S(2)}) collective-permute-start(bf16[768,256]{1,0:T(8,128)(2,1)S(1)} %add_convert_fusion.5), channel_id=1, source_target_pairs={{0,4},{4,0},{2,6},{6,2},{1,5},{5,1},{3,7},{7,3},{8,12},{12,8},{10,... | collective-permute-start | bytes 1179656 | tf_op jit(solution)/shard_map/ppermute | solution.py:41
  421.3 35.7 %collective-permute-start.49 = (bf16[768,1024]{1,0:T(8,128)(2,1)S(1)}, bf16[768,1024]{1,0:T(8,128)(2,1)S(1)}, u32[]{:S(2)}, u32[]{:S(2)}) collective-permute-start(bf16[768,1024]{1,0:T(8,128)(2,1)S(1)} %add_convert_fusion), channel_id=1, source_target_pairs={{0,1},{1,0},{2,3},{3,2},{4,5},{5,4},{6,7},{7,6},{8,9},{9,8},{10,11... | collective-permute-start | bytes 4718600 | tf_op jit(solution)/shard_map/ppermute | solution.py:51
  429.2 52.5 %collective-permute-start.56 = (bf16[4,2,64,2048]{3,2,0,1:T(8,128)(2,1)}, bf16[4,2,64,2048]{3,2,0,1:T(8,128)(2,1)}, u32[]{:S(2)}, u32[]{:S(2)}) collective-permute-start(bf16[4,2,64,2048]{3,2,0,1:T(8,128)(2,1)} %bitcast.166), channel_id=1, source_target_pairs={{0,2},{2,0},{4,6},{6,4},{1,3},{3,1},{5,7},{7,5},{8,10},{10,8},{12,... | collective-permute-start | bytes 6291464 | tf_op jit(solution)/shard_map/ppermute | solution.py:37
  488.4 33.3 %collective-permute-start.51 = (bf16[256,1024]{1,0:T(8,128)(2,1)S(1)}, bf16[256,1024]{1,0:T(8,128)(2,1)S(1)}, u32[]{:S(2)}, u32[]{:S(2)}) collective-permute-start(bf16[256,1024]{1,0:T(8,128)(2,1)S(1)} %slice_add_fusion), channel_id=1, source_target_pairs={{0,4},{4,0},{2,6},{6,2},{1,5},{5,1},{3,7},{7,3},{8,12},{12,8},{10,... | collective-permute-start | bytes 1572872 | tf_op jit(solution)/shard_map/ppermute | solution.py:41
  490.0 39.1 %collective-permute-start.39 = (bf16[256,1024]{1,0:T(8,128)(2,1)S(1)}, bf16[256,1024]{1,0:T(8,128)(2,1)S(1)}, u32[]{:S(2)}, u32[]{:S(2)}) collective-permute-start(bf16[256,1024]{1,0:T(8,128)(2,1)S(1)} %slice_add_fusion.2), channel_id=1, source_target_pairs={{0,4},{4,0},{2,6},{6,2},{1,5},{5,1},{3,7},{7,3},{8,12},{12,8},{10,... | collective-permute-start | bytes 1572872 | tf_op jit(solution)/shard_map/ppermute | solution.py:41
  (107 other events, 1963.3 us)
Sparse Core Ops, SparseCore 0:
  10.2 58.7 all-gather.2
  71.2 52.9 all-gather.4
  259.6 70.9 reduce-scatter.2
  334.9 74.2 reduce-scatter.4

commit v2 on v1

v2 whole, which is shorter than its diff:
```python
import functools
import math

import jax
import jax.numpy as jnp
from jax import lax
from jax.experimental import pallas as pl
from jax.experimental.pallas import tpu as pltpu
from jax.sharding import PartitionSpec as P

HD = 64
PAIR = 2 * HD
EPS = 1e-06
LOG2E = 1.4426950408889634
BF = jnp.bfloat16
F32 = jnp.float32
VMEM_LIMIT = 56 * 1024 * 1024
PAIRS_PER_CALL = 1
PARTS = 2
KEY_TILE = 512
QUERY_TILE = 256
HIDDEN_TILE = 256
WEIGHT = 4


def dot_nt(a, b):
    return lax.dot_general(a, b, (((1,), (1,)), ((), ())), preferred_element_type=F32)


def dot_tn(a, b):
    return lax.dot_general(a, b, (((0,), (0,)), ((), ())), preferred_element_type=F32)


def dot_nn(a, b):
    return jnp.dot(a, b, preferred_element_type=F32)


def swap_core(v):
    return lax.ppermute(v, "ctx", [(0, 1), (1, 0), (2, 3), (3, 2)])


def swap_y(v):
    return lax.ppermute(v, "ctx", [(0, 2), (2, 0), (1, 3), (3, 1)])


def after(v, *earlier):
    if not earlier:
        return v
    whole = pl.BlockSpec(memory_space=pl.ANY)
    return pl.pallas_call(
        lambda *refs: None,
        in_specs=[whole] * (1 + len(earlier)),
        out_specs=whole,
        out_shape=jax.ShapeDtypeStruct(v.shape, v.dtype),
        input_output_aliases={0: 0},
        name="after",
    )(v, *earlier)


def gather_ctx(v, over, *earlier):
    return v, over, swap_core(after(v, *earlier)), swap_core(after(over, *earlier))


def sum_tp(part, *earlier):
    if lax.axis_size("tp") == 2:
        other = after(lax.ppermute(part, "tp", [(0, 1), (1, 0)]), *earlier)
        return part.astype(F32) + other.astype(F32)
    return after(lax.psum(part, "tp"), *earlier).astype(F32)


def swap_line(v, bit):
    return lax.ppermute(v, "dp", [(i, i ^ bit) for i in range(lax.axis_size("dp"))])


def line_bits():
    return [1 << k for k in reversed(range(lax.axis_size("dp").bit_length() - 1))]


def gather_line(v, *earlier):
    z = lax.axis_index("dp")
    v = v[None]
    for stage, bit in enumerate(line_bits()):
        if stage:
            v = after(v, *earlier)
        other = swap_line(v, bit)
        odd = (z & bit) != 0
        pair = jnp.stack([jnp.where(odd, other, v), jnp.where(odd, v, other)], axis=1)
        v = pair.reshape(-1, *v.shape[1:])
    return v


def gather_rest(v, over, *earlier):
    me = lax.axis_index("ctx")
    odd_core, odd_y = (me & 1) == 1, (me >> 1) == 1
    b0, b2, b1, b3 = gather_ctx(v, over, *earlier)
    lo, hi = jnp.where(odd_core, b1, b0), jnp.where(odd_core, b0, b1)
    lo_far, hi_far = jnp.where(odd_core, b3, b2), jnp.where(odd_core, b2, b3)
    whole = jnp.stack(
        [
            jnp.where(odd_y, lo_far, lo),
            jnp.where(odd_y, hi_far, hi),
            jnp.where(odd_y, lo, lo_far),
            jnp.where(odd_y, hi, hi_far),
        ],
        axis=1,
    )
    return whole.reshape(-1, v.shape[2])


def scatter_stages(v, waits):
    n = lax.axis_size("dp")
    me = lax.axis_index("ctx")
    z = lax.axis_index("dp")
    rows, columns = v.shape
    v = v.reshape(n, 2, 2, rows // (4 * n), columns)

    waits = iter(waits)

    def halve(a, i, axis, swap):
        keep = lax.dynamic_index_in_dim(a, i, axis, keepdims=False)
        send = lax.dynamic_index_in_dim(a, 1 - i, axis, keepdims=False)
        other = after(swap(send), *next(waits, []))
        return keep.astype(F32) + other.astype(F32)

    v = halve(v, me & 1, 2, swap_core).astype(BF)
    yield v
    v = halve(v, me >> 1, 1, swap_y)
    bit = 1
    while bit < n:
        v = v.astype(BF)
        yield v
        v = v.reshape(v.shape[0] // 2, 2, *v.shape[1:])
        v = halve(v, (z // bit) & 1, 1, functools.partial(swap_line, bit=bit))
        bit *= 2
    yield v[0]


def sum_stages(v):
    v = v + swap_core(v)
    yield v
    v = v + swap_y(v)
    yield v
    for bit in line_bits():
        v = v + swap_line(v, bit)
        yield v


def attend_kernel(scale, q_ref, k0, k1, k2, k3, *refs):
    o_ref, low_ref, lse_ref = refs[-3:]
    rows = q_ref.shape[0]
    tile = min(QUERY_TILE, rows)
    first = lax.broadcasted_iota(jnp.int32, (1, PAIR), 1) < HD

    def step(i, carry):
        at = pl.ds(pl.multiple_of(i * tile, tile), tile)
        q = q_ref[at, :]
        outs = []
        for h in range(2):
            mine = first if h == 0 else jnp.logical_not(first)
            q_h = jnp.where(mine, q, jnp.zeros_like(q))
            scores = [dot_nt(q_h, k[:, :PAIR]) for k in (k0, k1, k2, k3)]
            top = functools.reduce(
                jnp.maximum, [jnp.max(s, axis=1, keepdims=True) for s in scores]
            )
            acc = None
            for s, k in zip(scores, (k0, k1, k2, k3)):
                p = jnp.exp2((s - top) * scale).astype(BF)
                v = k[:, PAIR:]
                term = dot_nn(p, jnp.where(mine, v, jnp.ones_like(v)))
                acc = term if acc is None else acc + term
            total = pltpu.roll(acc, HD, 1)
            outs.append(acc / total)
            lse = jnp.transpose(top * scale + jnp.log2(total))
            lse_ref[0, pl.ds(h, 1), at] = lse[h * HD : h * HD + 1, :]
        out = jnp.where(first, outs[0], outs[1])
        o_ref[at, :] = out
        low_ref[at, :] = out.astype(BF)
        return carry

    lax.fori_loop(0, rows // tile, step, 0)


def key_specs(rows):
    return [pl.BlockSpec((rows, 2 * PAIR), lambda i: (0, i))] * 4


def attend(q, blocks, call, calls, held, *earlier):
    rows, all_width = q.shape
    width = all_width // calls
    pairs = width // PAIR
    base = call * pairs
    keys = 4 * rows
    spec = pl.BlockSpec((rows, PAIR), lambda i: (0, base + i))
    return pl.pallas_call(
        functools.partial(attend_kernel, LOG2E / math.sqrt(HD)),
        grid=(pairs,),
        in_specs=[spec]
        + key_specs(rows)
        + [pl.BlockSpec(memory_space=pl.ANY)] * (len(held) + len(earlier)),
        out_specs=[spec, spec, pl.BlockSpec((1, 8, rows), lambda i: (base + i, 0, 0))],
        out_shape=[
            jax.ShapeDtypeStruct((rows, all_width), F32),
            jax.ShapeDtypeStruct((rows, all_width), BF),
            jax.ShapeDtypeStruct((calls * pairs, 8, rows), F32),
        ],
        input_output_aliases={5 + i: i for i in range(len(held))},
        cost_estimate=pl.CostEstimate(
            flops=(16 * rows * keys * width) // WEIGHT,
            bytes_accessed=(rows * width * 16) // WEIGHT,
            transcendentals=(rows * keys * width // HD) // WEIGHT,
        ),
        compiler_params=pltpu.CompilerParams(vmem_limit_bytes=VMEM_LIMIT),
        name="attend",
    )(q, *blocks, *held, *earlier)


def attend_back_kernel(scale, factor, blocks, last, q_ref, d_ref, o_ref, lse_ref, *refs):
    rows = q_ref.shape[0]
    keys = 2 * rows
    tile = min(KEY_TILE, rows)
    kv = refs[-2]
    dq_turned = refs[-1]
    dq_ref, out_ref = refs[-4:-2]
    start = 0
    for block in refs[:blocks]:
        kv[start : start + block.shape[0], :] = block[...]
        start += block.shape[0]
    first = lax.broadcasted_iota(jnp.int32, (1, PAIR), 1) < HD
    d = d_ref[...]
    q = q_ref[...]
    prod = jnp.transpose(d.astype(F32) * o_ref[...])
    halves = []
    for h in range(2):
        mine = first if h == 0 else jnp.logical_not(first)
        halves.append((
            jnp.where(mine, q, jnp.zeros_like(q)),
            jnp.where(mine, d, jnp.zeros_like(d)),
            lse_ref[0, h : h + 1, :],
            jnp.sum(prod[h * HD : (h + 1) * HD, :], axis=0, keepdims=True),
        ))
    dq_turned[...] = refs[blocks][...] if last else jnp.zeros_like(dq_turned)

    def step(i, carry):
        at = pl.ds(pl.multiple_of(i * tile, tile), tile)
        k = kv[at, :PAIR]
        v = kv[at, PAIR:]
        k_turned = jnp.transpose(k)
        dk = dv = None
        for h, (q_h, d_h, lse, delta) in enumerate(halves):
            prob = jnp.exp2(dot_nt(k, q_h) * scale - lse)
            d_score = (prob * (dot_nt(v, d_h) - delta)).astype(BF)
            dv_h = dot_nn(prob.astype(BF), d_h)
            dk_h = dot_nn(d_score, q_h)
            dv = dv_h if dv is None else dv + dv_h
            dk = dk_h if dk is None else dk + dk_h
            part = slice(h * HD, (h + 1) * HD)
            dq_turned[part, :] += dot_nn(k_turned[part, :], d_score)
        out_ref[at, :PAIR] = (dk * factor).astype(BF)
        out_ref[at, PAIR:] = dv.astype(BF)
        return carry

    lax.fori_loop(0, keys // tile, step, 0)
    if last:
        dq_ref[...] = (jnp.transpose(dq_turned[...]) * factor).astype(BF)
    else:
        dq_ref[...] = dq_turned[...]


def attend_back(q, d_att, o, lse, blocks, call, partial, *earlier):
    rows = q.shape[0]
    width = blocks[0].shape[1] // 2
    pairs = width // PAIR
    base = call * pairs
    keys = 2 * rows
    last = partial is not None
    wide = pl.BlockSpec((rows, PAIR), lambda i: (0, base + i))
    narrow = pl.BlockSpec((rows, PAIR), lambda i: (0, i))
    turned = pl.BlockSpec((PAIR, rows), lambda i: (i, 0))
    held = [partial] if last else []
    return pl.pallas_call(
        functools.partial(
            attend_back_kernel, LOG2E / math.sqrt(HD), 1.0 / math.sqrt(HD), len(blocks), last
        ),
        grid=(pairs,),
        in_specs=[wide, wide, wide, pl.BlockSpec((1, 8, rows), lambda i: (base + i, 0, 0))]
        + [pl.BlockSpec((b.shape[0], 2 * PAIR), lambda i: (0, i)) for b in blocks]
        + [turned] * len(held)
        + [pl.BlockSpec(memory_space=pl.ANY)] * len(earlier),
        out_specs=[
            narrow if last else turned,
            pl.BlockSpec((keys, 2 * PAIR), lambda i: (0, i)),
        ],
        out_shape=[
            jax.ShapeDtypeStruct((rows, width), BF)
            if last
            else jax.ShapeDtypeStruct((width, rows), F32),
            jax.ShapeDtypeStruct((keys, 2 * width), BF),
        ],
        scratch_shapes=[
            pltpu.VMEM((keys, 2 * PAIR), BF),
            pltpu.VMEM((PAIR, rows), F32),
        ],
        cost_estimate=pl.CostEstimate(
            flops=(40 * rows * keys * width) // WEIGHT,
            bytes_accessed=(rows * width * 40) // WEIGHT,
            transcendentals=(rows * keys * width // HD) // WEIGHT,
        ),
        compiler_params=pltpu.CompilerParams(vmem_limit_bytes=VMEM_LIMIT),
        name="attend_back",
    )(q, d_att, o, lse, *blocks, *held, *earlier)


def mlp_kernel(h2_ref, d_ref, in_ref, down_ref, bias_ref, *refs):
    pair_ref, y_ref, back_ref, bias_grad_ref, y_acc, back_acc = refs[-6:]
    i = pl.program_id(0)
    w_in, w_down = in_ref[...], down_ref[...]
    pre = dot_nn(h2_ref[...], w_in) + bias_ref[...]
    d_act = dot_nn(d_ref[...], w_down)
    below = 0.5 * (1.0 + lax.erf(pre * math.sqrt(0.5)))
    act = (pre * below).astype(BF)
    slope = below + pre * (jnp.exp(-0.5 * pre * pre) * (1.0 / math.sqrt(2.0 * math.pi)))
    d_pre = (d_act * slope).astype(BF)
    pair_ref[0] = d_pre
    pair_ref[1] = act
    bias_grad_ref[...] = jnp.sum(d_pre.astype(F32), axis=0, keepdims=True)
    y = dot_nt(act, w_down)
    back = dot_nt(d_pre, w_in)

    @pl.when(i == 0)
    def _():
        y_acc[...] = y
        back_acc[...] = back

    @pl.when(i > 0)
    def _():
        y_acc[...] += y
        back_acc[...] += back

    @pl.when(i == pl.num_programs(0) - 1)
    def _():
        y_ref[...] = y_acc[...].astype(BF)
        back_ref[...] = back_acc[...].astype(BF)


def mlp(h2, d_down, weights, bias, held, part, parts):
    rows, width = h2.shape
    hidden = bias.shape[1]
    tile = min(HIDDEN_TILE, hidden)
    tiles = hidden // tile
    whole = pl.BlockSpec((rows, width), lambda i: (0, 0))
    mine = pl.BlockSpec((rows, width), lambda i: (part, 0))
    w_in = pl.BlockSpec((width, tile), lambda i: (0, i))
    w_down = pl.BlockSpec((width, tile), lambda i: (0, tiles + i))
    line = pl.BlockSpec((1, tile), lambda i: (0, i))
    more = () if held is None else (held,)
    return pl.pallas_call(
        mlp_kernel,
        grid=(tiles,),
        in_specs=[whole, mine, w_in, w_down, line]
        + [pl.BlockSpec(memory_space=pl.ANY)] * len(more),
        out_specs=[pl.BlockSpec((2, rows, tile), lambda i: (0, part, i)), whole, whole, line],
        out_shape=[
            jax.ShapeDtypeStruct((2, rows * parts, hidden), BF),
            jax.ShapeDtypeStruct((rows, width), BF),
            jax.ShapeDtypeStruct((rows, width), BF),
            jax.ShapeDtypeStruct((1, hidden), F32),
        ],
        scratch_shapes=[pltpu.VMEM((rows, width), F32), pltpu.VMEM((rows, width), F32)],
        input_output_aliases={5: 0} if more else {},
        cost_estimate=pl.CostEstimate(
            flops=(8 * rows * width * hidden) // WEIGHT,
            bytes_accessed=(4 * width * hidden + 4 * rows * hidden + 8 * rows * width) // WEIGHT,
            transcendentals=(rows * hidden) // WEIGHT,
        ),
        compiler_params=pltpu.CompilerParams(vmem_limit_bytes=VMEM_LIMIT),
        name="mlp",
    )(h2, d_down, weights, weights, bias, *more)


def norm_parts(v):
    mean = jnp.mean(v, axis=-1, keepdims=True)
    centred = v - mean
    var = jnp.mean(centred * centred, axis=-1, keepdims=True)
    rstd = lax.rsqrt(var + EPS)
    return centred * rstd, rstd


def norm_back(d, unit, rstd, gain):
    d_unit = d * gain
    return rstd * (
        d_unit
        - jnp.mean(d_unit, axis=-1, keepdims=True)
        - unit * jnp.mean(d_unit * unit, axis=-1, keepdims=True)
    )


def body(
    tokens,
    lengths,
    norm_gain,
    norm_bias,
    qkv_weight,
    qv_bias,
    out_weight,
    mlp_in,
    mlp_bias,
    mlp_out,
    out_bias,
    cotangent,
):
    _, cap, width = tokens.shape
    n_ctx = lax.axis_size("ctx")
    slots = n_ctx * cap
    rows = 3 * slots // 4 // n_ctx
    spare = cap - rows
    local = qkv_weight.shape[2]
    hidden = mlp_in.shape[1]
    share = qkv_weight.shape[0]
    pairs = local // PAIR
    per_call = min(PAIRS_PER_CALL, pairs)
    calls = pairs // per_call
    me = lax.axis_index("ctx")

    small = jnp.concatenate([norm_gain, norm_bias, out_bias], axis=0)
    small = jnp.pad(small.T, ((0, 0), (0, PAIR - small.shape[0])))
    w_kv = jnp.stack(
        [qkv_weight[:, 1].reshape(share, pairs, PAIR), qkv_weight[:, 2].reshape(share, pairs, PAIR)],
        axis=2,
    ).reshape(share, 2 * local)
    tokens_far = swap_y(tokens[0, rows:])
    line = gather_line(jnp.concatenate([qkv_weight[:, 0], w_kv, small], axis=1), tokens_far)
    over = jnp.maximum(lengths - rows, 0)
    lack = jnp.maximum(rows - lengths, 0)
    row = lax.iota(jnp.int32, rows)
    column = lax.iota(jnp.int32, n_ctx * spare)
    owner = (column // spare) ^ me
    slot = column % spare
    my_length = jnp.int32(0)
    my_lack_at = jnp.int32(0)
    source = jnp.full((n_ctx * spare,), -2, jnp.int32)
    over_at = lack_at = jnp.int32(0)
    for c in range(n_ctx):
        my_length = jnp.where(me == c, lengths[c], my_length)
        my_lack_at = jnp.where(me == c, lack_at, my_lack_at)
        source = jnp.where((owner == c) & (slot < over[c]), over_at + slot, source)
        over_at, lack_at = over_at + over[c], lack_at + lack[c]
    own = row < my_length
    need = jnp.where(own, -1, my_lack_at + row - my_length)
    source = source.reshape(n_ctx, spare)
    source = jnp.concatenate([source[0], source[2], source[1], source[3]])
    pick = (need[:, None] == source[None, :]).astype(BF)

    def take(v, over):
        blocks = jnp.concatenate(gather_ctx(v[rows:], over), axis=0)
        return jnp.where(own[:, None], v[:rows], dot_nn(pick, blocks).astype(BF))

    def give_near(v):
        blocks = dot_tn(pick[:, spare:], v).astype(BF)
        return v, blocks, swap_core(blocks[spare:])

    def give_far(v, blocks, got):
        back = swap_y(blocks[:spare] + got[spare:])
        kept = jnp.where(own[:, None], v, jnp.zeros_like(v))
        return jnp.concatenate([kept, got[:spare] + back], axis=0)[None], back

    x_low = take(tokens[0], tokens_far)
    x = x_low.astype(F32)
    unit_one, rstd_one = norm_parts(x)

    line = after(line, x_low)
    line_far = swap_y(line)
    rest = jnp.concatenate([mlp_in, mlp_out.T, out_weight.T], axis=1)
    rest = lax.all_gather(after(rest, line_far), ("dp", "ctx"), axis=0, tiled=True)
    w_out = rest[:, 2 * hidden :]
    first = gather_rest(line, line_far)
    w_q, w_kv, w_qkv = first[:, :local], first[:, local : 3 * local], first[:, : 3 * local]
    small = first[:, 3 * local : 3 * local + 6].T.astype(F32)
    gains, shifts, biases = small[0:2], small[2:4], small[4:6]
    h1 = (unit_one * gains[0] + shifts[0]).astype(BF)
    kv_bias = jnp.stack(
        [jnp.zeros((pairs, PAIR), F32), qv_bias[1].reshape(pairs, PAIR)], axis=1
    ).reshape(2 * local)
    query = (dot_nn(h1, w_q) + qv_bias[0]).astype(BF)
    kvs, far = [], []
    for call in range(calls):
        at = slice(call * per_call * 2 * PAIR, (call + 1) * per_call * 2 * PAIR)
        kvs.append((dot_nn(h1, w_kv[:, at]) + kv_bias[at]).astype(BF))
    held, far, kv_blocks = (), [], []
    for call in range(min(2, calls)):
        kvs[call] = after(kvs[call], *far)
        far.append(swap_y(kvs[call]))
    for call in range(calls):
        kv_blocks.append(gather_ctx(kvs[call], after(far[call], *held[2:])))
        held = attend(query, kv_blocks[call], call, calls, held)
        if call + 2 < calls:
            kvs[call + 2] = after(kvs[call + 2], held[2])
            far.append(swap_y(kvs[call + 2]))
    attn, attended, lse = held
    cot_far = swap_y(after(cotangent[0, rows:], far[-1]))
    d_down = take(cotangent[0], after(cot_far, lse))
    parts = PARTS
    mine = rows // parts
    pair = None
    x_one, y_parts, back_parts, h2, mlp_bias_grad = [], [], [], [], 0.0
    for part in range(parts):
        at = slice(part * mine, (part + 1) * mine)
        branch = sum_tp(dot_nt(attended[at], w_out).astype(BF), *y_parts)
        x_part = x[at] + (branch + biases[0])
        unit, rstd = norm_parts(x_part)
        h2_part = (unit * gains[1] + shifts[1]).astype(BF)
        pair, y_part, back_part, bias_part = mlp(
            h2_part, d_down, rest, mlp_bias[None], pair, part, parts
        )
        x_one.append(x_part)
        h2.append(h2_part)
        y_parts.append(y_part)
        back_parts.append(back_part)
        mlp_bias_grad = mlp_bias_grad + bias_part
    d_h2 = [sum_tp(v, y_parts[-1]) for v in back_parts[:-1]]
    sides = after(jnp.stack([jnp.concatenate(h2, axis=0), d_down]), *d_h2)
    grads = jnp.einsum("btd,btf->bdf", sides, pair, preferred_element_type=F32).astype(BF)
    d_h2.append(sum_tp(back_parts[-1], grads))
    grad_mlp = lax.psum_scatter(grads, ("dp", "ctx"), scatter_dimension=1, tiled=True)
    grad_in = grad_mlp[0].astype(F32)
    grad_down = grad_mlp[1].astype(F32).T

    d_x_one, d_att, gain_two, shift_two = [], [], 0.0, 0.0
    for part in range(parts):
        at = slice(part * mine, (part + 1) * mine)
        unit, rstd = norm_parts(x_one[part])
        d_part = d_down[at].astype(F32) + norm_back(d_h2[part], unit, rstd, gains[1])
        d_x_one.append(d_part)
        d_att.append(dot_nn(d_part.astype(BF), w_out).astype(BF))
        gain_two = gain_two + jnp.sum(d_h2[part] * unit, axis=0)
        shift_two = shift_two + jnp.sum(d_h2[part], axis=0)
    d_x_one = jnp.concatenate(d_x_one, axis=0)
    d_att = jnp.concatenate(d_att, axis=0)
    d_branch = d_x_one.astype(BF)
    grad_out = dot_tn(d_branch, attended).astype(BF)
    sums = [
        gain_two,
        shift_two,
        jnp.sum(d_branch.astype(F32), axis=0),
        jnp.sum(d_down.astype(F32), axis=0),
    ]

    d_query, d_kv = [], []
    earlier = [grads]
    result_back = []
    for call in range(calls):
        near, over, *side = kv_blocks[call]
        partial, send = attend_back(query, d_att, attn, lse, side, call, None, *earlier)
        got = swap_core(send)
        dq, keep = attend_back(query, d_att, attn, lse, (near, over), call, partial)
        if call == calls - 1 and call > 2:
            got = after(got, result_back)
        got = after(got, keep)
        if call == min(1, calls - 1):
            result = give_near(
                jnp.concatenate([
                    (x_part + (sum_tp(after(y_part, d_att), keep) + biases[1])).astype(BF)
                    for x_part, y_part in zip(x_one, y_parts)
                ])
            )
        if call == min(2, calls - 1):
            result, result_back = give_far(*result[:2], after(result[2], keep))
        mid = (keep[rows:].astype(F32) + got[rows:].astype(F32)).astype(BF)
        far_kv = swap_y(mid)
        d_kv.append((keep[:rows], got[:rows], far_kv))
        d_query.append(dq)
        earlier = [mid]
        if call == min(1, calls - 1):
            earlier.append(result[2])
        if call == min(2, calls - 1):
            earlier.append(grad_mlp)
    d_kv = [
        (a.astype(F32) + b.astype(F32) + c.astype(F32)).astype(BF) for a, b, c in d_kv
    ]
    d_qkv = jnp.concatenate(d_query + d_kv, axis=1)
    qkv_sum = jnp.sum(d_qkv.astype(F32), axis=0)
    v_sum = qkv_sum[local:].reshape(pairs, 2, PAIR)[:, 1].reshape(local)
    few = sum_stages(
        jnp.concatenate([qkv_sum[:local], v_sum, mlp_bias_grad[0]]).reshape(-1, PAIR)
    )
    attn_back = dot_nt(d_qkv, w_qkv)
    sums = [jnp.sum(attn_back * unit_one, axis=0), jnp.sum(attn_back, axis=0), *sums]
    sums = jnp.pad(jnp.stack(sums), ((0, PAIR - len(sums)), (0, 0))).T
    grad_attn = jnp.concatenate(
        [dot_tn(h1, d_qkv).astype(BF), grad_out, sums.astype(BF)], axis=1
    )
    attn_low = attn_back.astype(BF)
    waits = [[], [], [], []]
    scatter = scatter_stages(grad_attn, waits)
    next(scatter)
    d_h1 = sum_tp(attn_low, next(scatter))
    grad_rows = (d_x_one + norm_back(d_h1, unit_one, rstd_one, gains[0])).astype(BF)
    rows_back, blocks, got = give_near(grad_rows)
    grad_tokens, tokens_back = give_far(rows_back, blocks, got)
    waits[3].append(tokens_back)
    waits[2].append(grad_rows)
    for few_sums in few:
        pass
    few_sums = few_sums.reshape(-1)
    for grad_attn in scatter:
        pass
    grad_qkv = grad_attn[:, : 3 * local]
    grad_out = grad_attn[:, 3 * local : 4 * local].T
    sums = grad_attn[:, 4 * local : 4 * local + 6].T
    ones = sums[:2]
    if lax.axis_size("tp") == 2:
        ones = ones + lax.ppermute(ones, "tp", [(0, 1), (1, 0)])
    else:
        ones = lax.psum(ones, "tp")
    grad_kv = grad_qkv[:, local:].reshape(share, pairs, 2, PAIR)
    grad_qkv = jnp.stack(
        [
            grad_qkv[:, :local],
            grad_kv[:, :, 0].reshape(share, local),
            grad_kv[:, :, 1].reshape(share, local),
        ],
        axis=1,
    )

    grad_gain = jnp.stack([ones[0], sums[2]])
    grad_shift = jnp.stack([ones[1], sums[3]])
    grad_out_bias = sums[4:6]
    qv_grad = few_sums[: 2 * local].reshape(2, local)
    mlp_bias_sum = few_sums[2 * local :]
    return (
        result,
        grad_tokens,
        grad_gain,
        grad_shift,
        grad_qkv,
        qv_grad,
        grad_out,
        grad_in,
        mlp_bias_sum,
        grad_down,
        grad_out_bias,
    )


def solution(mesh):
    in_specs = (
        P("dp", "ctx", None),
        P(),
        P(None, ("dp", "ctx")),
        P(None, ("dp", "ctx")),
        P(("dp", "ctx"), None, "tp"),
        P(None, "tp"),
        P("tp", ("dp", "ctx")),
        P(("dp", "ctx"), "tp"),
        P("tp"),
        P("tp", ("dp", "ctx")),
        P(None, ("dp", "ctx")),
        P("dp", "ctx", None),
    )
    out_specs = (
        P("dp", "ctx", None),
        P("dp", "ctx", None),
        P(None, ("dp", "ctx")),
        P(None, ("dp", "ctx")),
        P(("dp", "ctx"), None, "tp"),
        P(None, "tp"),
        P("tp", ("dp", "ctx")),
        P(("dp", "ctx"), "tp"),
        P("tp"),
        P("tp", ("dp", "ctx")),
        P(None, ("dp", "ctx")),
    )
    return jax.shard_map(body, mesh=mesh, in_specs=in_specs, out_specs=out_specs, check_vma=False)
```

time: 568 us -> 535 us (0.942)
  waiting for transfers between devices: 221 us -> 150 us
  starting transfers between devices: 79.9 us -> 36.9 us
  other arithmetic: 58 us -> 80.6 us
  local copies, waits for them, and re-layouts: 19.6 us -> 42 us
  matrix products: 38.8 us -> 54.4 us
  Pallas kernels: 130 us -> 143 us
  between operations: 15.8 us -> 22.8 us
    ppermute x24 -> x14, waiting for transfers between devices: 119 us -> 58.8 us  [the longest x7 36.8 us: sum_tp(): other = after(lax.ppermute(part, 'tp', [(0, 1), (1, 0)]), *earlier)]
    ppermute x24 -> x14, starting transfers between devices: 52.8 us -> 19.2 us  [the longest x6 11.6 us: swap_line(): lax.ppermute(v, 'dp', [(i, i ^ bit) for i in range(lax.axis_size('dp'))])]
    ppermute x16 -> x15, waiting for transfers between devices: 99.8 us -> 79.6 us  [swap_y(): return lax.ppermute(v, 'ctx', [(0, 2), (2, 0), (1, 3), (3, 1)])]
    unnamed x148 -> x194, local copies, waits for them, and re-layouts: 5.27 us -> 21 us
    dot_general x7 -> x4, matrix products: 23.8 us -> 11 us  [dot_tn(): lax.dot_general(a, b, (((0,), (0,)), ((), ())), preferred_element_type=F32)]
    dot_general x8 -> x9, matrix products: 11.1 us -> 23.4 us  [dot_nn(): return jnp.dot(a, b, preferred_element_type=F32)]
    dot_general x0 -> x1, matrix products: none -> 12.3 us  [body(): jnp.einsum('btd,btf->bdf', sides, pair, preferred_element_type=F32)]
    ppermute x24 -> x22, waiting for transfers between devices: 2.2 us -> 11.9 us  [swap_core(): return lax.ppermute(v, 'ctx', [(0, 1), (1, 0), (2, 3), (3, 2)])]
  transfers between devices with their start and end apart: 68 -> 53, of which waited for: 28 -> 21; matrix products, arithmetic and copies ran while one was open for 18% -> 21% of each run, Pallas kernels for 18% -> 27%
where the time goes in v2:
time: 535 us; the launch traced here: 530 us
  waiting for transfers between devices  150 us (28%)
  Pallas kernels  143 us (27%)
  other arithmetic  80.6 us (15%)
  matrix products  54.4 us (10%)
  local copies, waits for them, and re-layouts  42 us (8%)
  starting transfers between devices  36.9 us (7%)
  between operations  22.8 us (4%)
    ppermute x15, waiting for transfers between devices, swap_y(): return lax.ppermute(v, 'ctx', [(0, 2), (2, 0), (1, 3), (3, 1)])  79.6 us
    pallas_call x8, Pallas kernels, attend_back(): pl.pallas_call(functools.partial(attend_back_kernel, LOG2E / math.sqrt(HD...  73.2 us
    pallas_call x4, Pallas kernels, attend(): pl.pallas_call(functools.partial(attend_kernel, LOG2E / math.sqrt(HD)), g...  38.8 us
    ppermute x7, waiting for transfers between devices, sum_tp(): other = after(lax.ppermute(part, 'tp', [(0, 1), (1, 0)]), *earlier)  36.8 us
    pallas_call x2, Pallas kernels, mlp(): pl.pallas_call(mlp_kernel, grid=(tiles,), in_specs=[whole, mine, w_in, w_...  31 us
    dot_general x9, matrix products, dot_nn(): return jnp.dot(a, b, preferred_element_type=F32)  23.4 us
    ppermute x6, waiting for transfers between devices, swap_line(): lax.ppermute(v, 'dp', [(i, i ^ bit) for i in range(lax.axis_size('dp'))])  22 us
    unnamed x194, local copies, waits for them, and re-layouts  21 us
  transfers between devices with their start and end apart: 53, of which 21 were waited for; matrix products, arithmetic and copies ran while one was open for 21% of the time, Pallas kernels for 27%

profile of v2, /device:TPU:0, one launch (start us, length us, event | category | flops | bytes accessed | tf_op | source)
XLA Modules:
  0.0 530.0 jit_solution(3930768853734704929)
XLA Ops:
  30.0 10.5 %collective-permute-done.4 = bf16[2,64,1664]{2,1,0:T(8,128)(2,1)S(1)} collective-permute-done((bf16[2,64,1664]{2,1,0:T(8,128)(2,1)}, bf16[2,64,1664]{2,1,0:T(8,128)(2,1)S(1)}, u32[]{:S(2)}, u32[]{:S(2)}) %collective-permute-start.4) | collective-permute-done | bytes 426016 | tf_op jit(solution)/shard_map/ppermute | solution.py:72
  49.4 17.8 %collective-permute-done.5.refs_1_ = bf16[4,64,1664]{2,1,0:T(8,128)(2,1)S(1)} collective-permute-done((bf16[4,64,1664]{2,1,0:T(8,128)(2,1)}, bf16[4,64,1664]{2,1,0:T(8,128)(2,1)S(1)}, u32[]{:S(2)}, u32[]{:S(2)}) %collective-permute-start.5) | collective-permute-done | bytes 852000 | tf_op jit(solution)/shard_map/ppermute | solution.py:43
  79.5 13.7 %collective-permute-done.8.refs_1_.k1 = bf16[768,256]{1,0:T(8,128)(2,1)S(1)} collective-permute-done((bf16[768,256]{1,0:T(8,128)(2,1)}, bf16[768,256]{1,0:T(8,128)(2,1)S(1)}, u32[]{:S(2)}, u32[]{:S(2)}) %collective-permute-start.8) | collective-permute-done | bytes 393248 | tf_op jit(solution)/shard_map/ppermute | solution.py:43
  100.2 9.6 %attend.4 = (f32[768,512]{1,0:T(8,128)}, bf16[768,512]{1,0:T(8,128)(2,1)}, f32[4,8,768]{2,1,0:T(8,128)}) custom-call(bf16[768,512]{1,0:T(8,128)(2,1)} %add_convert_fusion.6.q_ref, bf16[768,256]{1,0:T(8,128)(2,1)} %fusion.48.k0.refs_0_, bf16[768,256]{1,0:T(8,128)(2,1)} %copy-done.65, bf16[768,256]{1,0:T(8,128)(2,1)} %copy-done.61, bf16[768,256]{1,0:T(8,128)(2,1)} %copy-done.62), custom_call_target="tpu_custom_call" | custom-call | flops 1207959552 | bytes 393216 | tf_op jit(solution)/shard_map/attend/pallas_call | solution.py:194
  118.0 9.6 %attend.5 = (f32[768,512]{1,0:T(8,128)}, bf16[768,512]{1,0:T(8,128)(2,1)}, f32[4,8,768]{2,1,0:T(8,128)}) custom-call(bf16[768,512]{1,0:T(8,128)(2,1)} %add_convert_fusion.6.q_ref, bf16[768,256]{1,0:T(8,128)(2,1)} %after.30.k0.refs_0_, bf16[768,256]{1,0:T(8,128)(2,1)} %after.31.k1.refs_1_, ...), custom_call_target="tpu_custom_call", output_to_operand_aliasing={{0}: (5, {}), {1}: (6, {}), {2}: (7, {})} | custom-call | flops 1207959552 | bytes 393216 | tf_op jit(solution)/shard_map/attend/pallas_call | solution.py:194
  128.0 6.5 %collective-permute-done.15.refs_0_ = bf16[768,256]{1,0:T(8,128)(2,1)S(1)} collective-permute-done((bf16[768,256]{1,0:T(8,128)(2,1)}, bf16[768,256]{1,0:T(8,128)(2,1)S(1)}, u32[]{:S(2)}, u32[]{:S(2)}) %collective-permute-start.15) | collective-permute-done | bytes 393248 | tf_op jit(solution)/shard_map/ppermute | solution.py:43
  137.6 10.8 %collective-permute-done.14.refs_0_.refs_1_ = bf16[768,256]{1,0:T(8,128)(2,1)S(1)} collective-permute-done((bf16[768,256]{1,0:T(8,128)(2,1)}, bf16[768,256]{1,0:T(8,128)(2,1)S(1)}, u32[]{:S(2)}, u32[]{:S(2)}) %collective-permute-start.14) | collective-permute-done | bytes 393248 | tf_op jit(solution)/shard_map/ppermute | solution.py:43
  149.5 9.8 %attend.6 = (f32[768,512]{1,0:T(8,128)}, bf16[768,512]{1,0:T(8,128)(2,1)}, f32[4,8,768]{2,1,0:T(8,128)}) custom-call(bf16[768,512]{1,0:T(8,128)(2,1)} %add_convert_fusion.6.q_ref, bf16[768,256]{1,0:T(8,128)(2,1)} %after.33.k0.refs_0_, bf16[768,256]{1,0:T(8,128)(2,1)} %after.34.k1.refs_1_, ...), custom_call_target="tpu_custom_call", output_to_operand_aliasing={{0}: (5, {}), {1}: (6, {}), {2}: (7, {})} | custom-call | flops 1207959552 | bytes 393216 | tf_op jit(solution)/shard_map/attend/pallas_call | solution.py:194
  162.5 9.7 %attend.7 = (f32[768,512]{1,0:T(8,128)}, bf16[768,512]{1,0:T(8,128)(2,1)}, f32[4,8,768]{2,1,0:T(8,128)}) custom-call(bf16[768,512]{1,0:T(8,128)(2,1)} %add_convert_fusion.6.q_ref, bf16[768,256]{1,0:T(8,128)(2,1)} %after.32.k0.refs_0_, bf16[768,256]{1,0:T(8,128)(2,1)} %after.35.k1.refs_1_, ...), custom_call_target="tpu_custom_call", output_to_operand_aliasing={{0}: (5, {}), {1}: (6, {}), {2}: (7, {})} | custom-call | flops 1207959552 | bytes 393216 | tf_op jit(solution)/shard_map/attend/pallas_call | solution.py:194
  185.7 12.0 %collective-permute-done.20 = bf16[384,1024]{1,0:T(8,128)(2,1)S(1)} collective-permute-done((bf16[384,1024]{1,0:T(8,128)(2,1)S(1)}, bf16[384,1024]{1,0:T(8,128)(2,1)S(1)}, u32[]{:S(2)}, u32[]{:S(2)}) %collective-permute-start.20) | collective-permute-done | bytes 786464 | tf_op jit(solution)/shard_map/ppermute | solution.py:66
  199.6 15.3 %mlp.2 = (bf16[2,768,2048]{2,1,0:T(8,128)(2,1)}, bf16[384,1024]{1,0:T(8,128)(2,1)}, bf16[384,1024]{1,0:T(8,128)(2,1)}, f32[1,2048]{1,0:T(1,128)}) custom-call(bf16[384,1024]{1,0:T(8,128)(2,1)} %add_convert_fusion.5.h2_ref, bf16[768,1024]{1,0:T(8,128)(2,1)} %get-tuple-element.210.d_ref, bf16[1024,4608]{1,0:T(8,128)(2,1)} %all-gather.2.cloned.1.call-done.in_ref.down_ref, ...), custom_call_target="tpu_custom_call" | custom-call | flops 1610612736 | bytes 3670016 | tf_op jit(solution)/shard_map/mlp/pallas_call | solution.py:356
  221.5 15.7 %mlp.3 = (bf16[2,768,2048]{2,1,0:T(8,128)(2,1)}, bf16[384,1024]{1,0:T(8,128)(2,1)}, bf16[384,1024]{1,0:T(8,128)(2,1)}, f32[1,2048]{1,0:T(1,128)}) custom-call(bf16[384,1024]{1,0:T(8,128)(2,1)} %add_convert_fusion.4.h2_ref, bf16[768,1024]{1,0:T(8,128)(2,1)} %get-tuple-element.210.d_ref, ...), custom_call_target="tpu_custom_call", output_to_operand_aliasing={{0}: (5, {})} | custom-call | flops 1610612736 | bytes 3670016 | tf_op jit(solution)/shard_map/mlp/pallas_call | solution.py:356
  243.8 12.3 %convolution_convert_fusion.refs_1_.refs_2_ = bf16[2,1024,2048]{2,1,0:T(8,128)(2,1)} fusion(bf16[2,768,1024]{2,1,0:T(8,128)(2,1)} %after.41, bf16[2,768,2048]{2,1,0:T(8,128)(2,1)} %get-tuple-element.63), kind=kOutput, calls=%fused_computation | convolution fusion | flops 6446645248 | bytes 17825792 | tf_op jit(solution)/shard_map/btd,btf->bdf/dot_general | solution.py:521
  256.5 18.4 %collective-permute-done.26.refs_0_ = bf16[384,1024]{1,0:T(8,128)(2,1)} collective-permute-done((bf16[384,1024]{1,0:T(8,128)(2,1)}, bf16[384,1024]{1,0:T(8,128)(2,1)}, u32[]{:S(2)}, u32[]{:S(2)}) %collective-permute-start.26) | collective-permute-done | bytes 786464 | tf_op jit(solution)/shard_map/ppermute | solution.py:66
  285.8 9.1 %attend_back.8 = (f32[128,768]{1,0:T(8,128)}, bf16[1536,256]{1,0:T(8,128)(2,1)}) custom-call(bf16[768,512]{1,0:T(8,128)(2,1)} %add_convert_fusion.6.q_ref, bf16[768,512]{1,0:T(8,128)(2,1)} %pad_maximum_fusion.7.refs_1_.d_ref, f32[768,512]{1,0:T(8,128)} %get-tuple-element.64.o_ref, f32[4,8,768]{2,1,0:T(8,128)} %get-tuple-element.57.refs_1_.lse_ref, ...), custom_call_target="tpu_custom_call" | custom-call | flops 1509949440 | bytes 983040 | tf_op jit(solution)/shard_map/attend_back/pallas_call | solution.py:280
  298.5 9.3 %attend_back.9 = (bf16[768,128]{1,0:T(8,128)(2,1)}, bf16[1536,256]{1,0:T(8,128)(2,1)}) custom-call(bf16[768,512]{1,0:T(8,128)(2,1)} %add_convert_fusion.6.q_ref, bf16[768,512]{1,0:T(8,128)(2,1)} %pad_maximum_fusion.7.refs_1_.d_ref, f32[768,512]{1,0:T(8,128)} %get-tuple-element.64.o_ref, f32[4,8,768]{2,1,0:T(8,128)} %get-tuple-element.57.refs_1_.lse_ref, ...), custom_call_target="tpu_custom_call" | custom-call | flops 1509949440 | bytes 983040 | tf_op jit(solution)/shard_map/attend_back/pallas_call | solution.py:280
  309.7 9.1 %attend_back.10 = (f32[128,768]{1,0:T(8,128)}, bf16[1536,256]{1,0:T(8,128)(2,1)}) custom-call(bf16[768,512]{1,0:T(8,128)(2,1)} %add_convert_fusion.6.q_ref, bf16[768,512]{1,0:T(8,128)(2,1)} %pad_maximum_fusion.7.refs_1_.d_ref, f32[768,512]{1,0:T(8,128)} %get-tuple-element.64.o_ref, f32[4,8,768]{2,1,0:T(8,128)} %get-tuple-element.57.refs_1_.lse_ref, ...), custom_call_target="tpu_custom_call" | custom-call | flops 1509949440 | bytes 983040 | tf_op jit(solution)/shard_map/attend_back/pallas_call | solution.py:280
  318.8 9.2 %attend_back.11 = (bf16[768,128]{1,0:T(8,128)(2,1)}, bf16[1536,256]{1,0:T(8,128)(2,1)}) custom-call(bf16[768,512]{1,0:T(8,128)(2,1)} %add_convert_fusion.6.q_ref, bf16[768,512]{1,0:T(8,128)(2,1)} %pad_maximum_fusion.7.refs_1_.d_ref, f32[768,512]{1,0:T(8,128)} %get-tuple-element.64.o_ref, f32[4,8,768]{2,1,0:T(8,128)} %get-tuple-element.57.refs_1_.lse_ref, ...), custom_call_target="tpu_custom_call" | custom-call | flops 1509949440 | bytes 983040 | tf_op jit(solution)/shard_map/attend_back/pallas_call | solution.py:280
  344.1 9.2 %attend_back.12 = (f32[128,768]{1,0:T(8,128)}, bf16[1536,256]{1,0:T(8,128)(2,1)}) custom-call(bf16[768,512]{1,0:T(8,128)(2,1)} %add_convert_fusion.6.q_ref, bf16[768,512]{1,0:T(8,128)(2,1)} %pad_maximum_fusion.7.refs_1_.d_ref, f32[768,512]{1,0:T(8,128)} %get-tuple-element.64.o_ref, f32[4,8,768]{2,1,0:T(8,128)} %get-tuple-element.57.refs_1_.lse_ref, ...), custom_call_target="tpu_custom_call" | custom-call | flops 1509949440 | bytes 983040 | tf_op jit(solution)/shard_map/attend_back/pallas_call | solution.py:280
  359.6 9.1 %attend_back.13 = (bf16[768,128]{1,0:T(8,128)(2,1)}, bf16[1536,256]{1,0:T(8,128)(2,1)}) custom-call(bf16[768,512]{1,0:T(8,128)(2,1)} %add_convert_fusion.6.q_ref, bf16[768,512]{1,0:T(8,128)(2,1)} %pad_maximum_fusion.7.refs_1_.d_ref, f32[768,512]{1,0:T(8,128)} %get-tuple-element.64.o_ref, f32[4,8,768]{2,1,0:T(8,128)} %get-tuple-element.57.refs_1_.lse_ref, ...), custom_call_target="tpu_custom_call" | custom-call | flops 1509949440 | bytes 983040 | tf_op jit(solution)/shard_map/attend_back/pallas_call | solution.py:280
  371.7 9.1 %attend_back.14 = (f32[128,768]{1,0:T(8,128)}, bf16[1536,256]{1,0:T(8,128)(2,1)}) custom-call(bf16[768,512]{1,0:T(8,128)(2,1)} %add_convert_fusion.6.q_ref, bf16[768,512]{1,0:T(8,128)(2,1)} %pad_maximum_fusion.7.refs_1_.d_ref, f32[768,512]{1,0:T(8,128)} %get-tuple-element.64.o_ref, f32[4,8,768]{2,1,0:T(8,128)} %get-tuple-element.57.refs_1_.lse_ref, ...), custom_call_target="tpu_custom_call" | custom-call | flops 1509949440 | bytes 983040 | tf_op jit(solution)/shard_map/attend_back/pallas_call | solution.py:280
  384.9 9.1 %attend_back.15 = (bf16[768,128]{1,0:T(8,128)(2,1)}, bf16[1536,256]{1,0:T(8,128)(2,1)}) custom-call(bf16[768,512]{1,0:T(8,128)(2,1)} %add_convert_fusion.6.q_ref, bf16[768,512]{1,0:T(8,128)(2,1)} %pad_maximum_fusion.7.refs_1_.d_ref, f32[768,512]{1,0:T(8,128)} %get-tuple-element.64.o_ref, f32[4,8,768]{2,1,0:T(8,128)} %get-tuple-element.57.refs_1_.lse_ref, ...), custom_call_target="tpu_custom_call" | custom-call | flops 1509949440 | bytes 983040 | tf_op jit(solution)/shard_map/attend_back/pallas_call | solution.py:280
  443.4 22.9 %collective-permute-done.48 = f32[24,128]{1,0:T(8,128)S(1)} collective-permute-done((f32[24,128]{1,0:T(8,128)S(1)}, f32[24,128]{1,0:T(8,128)S(1)}, u32[]{:S(2)}, u32[]{:S(2)}) %collective-permute-start.48) | collective-permute-done | bytes 12320 | tf_op jit(solution)/shard_map/ppermute | solution.py:43
  503.2 8.9 %collective-permute-done.45.refs_0_ = bf16[1,64,2176]{2,1,0:T(8,128)(2,1)S(1)} collective-permute-done((bf16[1,64,2176]{2,1,0:T(8,128)(2,1)S(1)}, bf16[1,64,2176]{2,1,0:T(8,128)(2,1)S(1)}, u32[]{:S(2)}, u32[]{:S(2)}) %collective-permute-start.45) | collective-permute-done | bytes 278560 | tf_op jit(solution)/shard_map/ppermute | solution.py:72
  (466 shorter events, 230.4 us)
Async XLA Ops:
  7.2 168.0 %all-gather.2.cloned.1.call-start = ((), (), s32[]{:S(2)}) async-start(), calls=%async_computation.1 | async-start | bytes 10027008 | tf_op jit(solution)/shard_map/all_gather | solution.py:473
  11.4 31.3 %collective-permute-start.1 = (bf16[256,1024]{1,0:T(8,128)(2,1)S(1)}, bf16[256,1024]{1,0:T(8,128)(2,1)S(1)}, u32[]{:S(2)}, u32[]{:S(2)}) collective-permute-start(bf16[256,1024]{1,0:T(8,128)(2,1)S(1)} %slice_bitcast_fusion.1), channel_id=1, source_target_pairs={{0,2},{2,0},{4,6},{6,4},{1,3},{3,1},{5,7},{7,5},{8,10},{10,8},{12,... | collective-permute-start | bytes 1572872 | tf_op jit(solution)/shard_map/ppermute | solution.py:39
  46.6 20.5 %collective-permute-start.5 = (bf16[4,64,1664]{2,1,0:T(8,128)(2,1)}, bf16[4,64,1664]{2,1,0:T(8,128)(2,1)S(1)}, u32[]{:S(2)}, u32[]{:S(2)}) collective-permute-start(bf16[4,64,1664]{2,1,0:T(8,128)(2,1)} %after.29), channel_id=1, source_target_pairs={{0,4},{4,0},{2,6},{6,2},{1,5},{5,1},{3,7},{7,3},{8,12},{12,8},{10,... | collective-permute-start | bytes 2555912 | tf_op jit(solution)/shard_map/ppermute | solution.py:43
  68.1 303.5 %reduce-scatter.2.cloned.1.call-start = ((), (), s32[]{:S(2)}) async-start(), calls=%async_computation.2 | async-start | bytes 8912896 | tf_op jit(solution)/shard_map/reduce_scatter | solution.py:523
  79.5 19.1 %collective-permute-start.10 = (bf16[768,256]{1,0:T(8,128)(2,1)}, bf16[768,256]{1,0:T(8,128)(2,1)S(1)}, u32[]{:S(2)}, u32[]{:S(2)}) collective-permute-start(bf16[768,256]{1,0:T(8,128)(2,1)} %fusion.48.k0.refs_0_), channel_id=1, source_target_pairs={{0,2},{2,0},{4,6},{6,4},{1,3},{3,1},{5,7},{7,5},{8,10},{10,8},{12,... | collective-permute-start | bytes 1179656 | tf_op jit(solution)/shard_map/ppermute | solution.py:39
  98.5 19.5 %collective-permute-start.12 = (bf16[768,256]{1,0:T(8,128)(2,1)}, bf16[768,256]{1,0:T(8,128)(2,1)}, u32[]{:S(2)}, u32[]{:S(2)}) collective-permute-start(bf16[768,256]{1,0:T(8,128)(2,1)} %after.30.k0.refs_0_), channel_id=1, source_target_pairs={{0,2},{2,0},{4,6},{6,4},{1,3},{3,1},{5,7},{7,5},{8,10},{10,8},{12,... | collective-permute-start | bytes 1179656 | tf_op jit(solution)/shard_map/ppermute | solution.py:39
  113.9 20.6 %collective-permute-start.15 = (bf16[768,256]{1,0:T(8,128)(2,1)}, bf16[768,256]{1,0:T(8,128)(2,1)S(1)}, u32[]{:S(2)}, u32[]{:S(2)}) collective-permute-start(bf16[768,256]{1,0:T(8,128)(2,1)} %after.33.k0.refs_0_), channel_id=1, source_target_pairs={{0,4},{4,0},{2,6},{6,2},{1,5},{5,1},{3,7},{7,3},{8,12},{12,8},{10,... | collective-permute-start | bytes 1179656 | tf_op jit(solution)/shard_map/ppermute | solution.py:43
  127.6 20.8 %collective-permute-start.14 = (bf16[768,256]{1,0:T(8,128)(2,1)}, bf16[768,256]{1,0:T(8,128)(2,1)S(1)}, u32[]{:S(2)}, u32[]{:S(2)}) collective-permute-start(bf16[768,256]{1,0:T(8,128)(2,1)} %after.32.k0.refs_0_), channel_id=1, source_target_pairs={{0,4},{4,0},{2,6},{6,2},{1,5},{5,1},{3,7},{7,3},{8,12},{12,8},{10,... | collective-permute-start | bytes 1179656 | tf_op jit(solution)/shard_map/ppermute | solution.py:43
  128.0 21.5 %collective-permute-start.16 = (bf16[768,256]{1,0:T(8,128)(2,1)}, bf16[768,256]{1,0:T(8,128)(2,1)}, u32[]{:S(2)}, u32[]{:S(2)}) collective-permute-start(bf16[768,256]{1,0:T(8,128)(2,1)} %after.33.k0.refs_0_), channel_id=1, source_target_pairs={{0,2},{2,0},{4,6},{6,4},{1,3},{3,1},{5,7},{7,5},{8,10},{10,8},{12,... | collective-permute-start | bytes 1179656 | tf_op jit(solution)/shard_map/ppermute | solution.py:39
  137.1 22.7 %collective-permute-start.18 = (bf16[768,256]{1,0:T(8,128)(2,1)S(1)}, bf16[768,256]{1,0:T(8,128)(2,1)S(1)}, u32[]{:S(2)}, u32[]{:S(2)}) collective-permute-start(bf16[768,256]{1,0:T(8,128)(2,1)S(1)} %copy-done.47), channel_id=1, source_target_pairs={{0,2},{2,0},{4,6},{6,4},{1,3},{3,1},{5,7},{7,5},{8,10},{10,8},{12,... | collective-permute-start | bytes 1179656 | tf_op jit(solution)/shard_map/ppermute | solution.py:39
  149.2 23.1 %collective-permute-start.21 = (bf16[256,1024]{1,0:T(8,128)(2,1)}, bf16[256,1024]{1,0:T(8,128)(2,1)S(1)}, u32[]{:S(2)}, u32[]{:S(2)}) collective-permute-start(bf16[256,1024]{1,0:T(8,128)(2,1)} %after.37), channel_id=1, source_target_pairs={{0,4},{4,0},{2,6},{6,2},{1,5},{5,1},{3,7},{7,3},{8,12},{12,8},{10,... | collective-permute-start | bytes 1572872 | tf_op jit(solution)/shard_map/ppermute | solution.py:43
  159.3 19.7 %collective-permute-start.22 = (bf16[256,1024]{1,0:T(8,128)(2,1)S(1)}, bf16[256,1024]{1,0:T(8,128)(2,1)}, u32[]{:S(2)}, u32[]{:S(2)}) collective-permute-start(bf16[256,1024]{1,0:T(8,128)(2,1)S(1)} %slice_bitcast_fusion), channel_id=1, source_target_pairs={{0,2},{2,0},{4,6},{6,4},{1,3},{3,1},{5,7},{7,5},{8,10},{10,8},{12,... | collective-permute-start | bytes 1572872 | tf_op jit(solution)/shard_map/ppermute | solution.py:39
  177.2 20.4 %collective-permute-start.20 = (bf16[384,1024]{1,0:T(8,128)(2,1)S(1)}, bf16[384,1024]{1,0:T(8,128)(2,1)S(1)}, u32[]{:S(2)}, u32[]{:S(2)}) collective-permute-start(bf16[384,1024]{1,0:T(8,128)(2,1)S(1)} %convolution_convert_fusion.4), channel_id=1, source_target_pairs={{0,1},{1,0},{2,3},{3,2},{4,5},{5,4},{6,7},{7,6},{8,9},{9,8},{10,11... | collective-permute-start | bytes 2359304 | tf_op jit(solution)/shard_map/ppermute | solution.py:66
  185.3 29.7 %collective-permute-start.25 = (bf16[384,1024]{1,0:T(8,128)(2,1)S(1)}, bf16[384,1024]{1,0:T(8,128)(2,1)S(1)}, u32[]{:S(2)}, u32[]{:S(2)}) collective-permute-start(bf16[384,1024]{1,0:T(8,128)(2,1)S(1)} %convolution_convert_fusion.3), channel_id=1, source_target_pairs={{0,1},{1,0},{2,3},{3,2},{4,5},{5,4},{6,7},{7,6},{8,9},{9,8},{10,11... | collective-permute-start | bytes 2359304 | tf_op jit(solution)/shard_map/ppermute | solution.py:66
  218.2 22.4 %collective-permute-start.24 = (bf16[384,1024]{1,0:T(8,128)(2,1)S(1)}, bf16[384,1024]{1,0:T(8,128)(2,1)}, u32[]{:S(2)}, u32[]{:S(2)}) collective-permute-start(bf16[384,1024]{1,0:T(8,128)(2,1)S(1)} %copy-done.37), channel_id=1, source_target_pairs={{0,1},{1,0},{2,3},{3,2},{4,5},{5,4},{6,7},{7,6},{8,9},{9,8},{10,11... | collective-permute-start | bytes 2359304 | tf_op jit(solution)/shard_map/ppermute | solution.py:66
  294.9 33.0 %collective-permute-start.29 = (bf16[384,1024]{1,0:T(8,128)(2,1)}, bf16[384,1024]{1,0:T(8,128)(2,1)}, u32[]{:S(2)}, u32[]{:S(2)}) collective-permute-start(bf16[384,1024]{1,0:T(8,128)(2,1)} %after.46), channel_id=1, source_target_pairs={{0,1},{1,0},{2,3},{3,2},{4,5},{5,4},{6,7},{7,6},{8,9},{9,8},{10,11... | collective-permute-start | bytes 2359304 | tf_op jit(solution)/shard_map/ppermute | solution.py:66
  295.4 36.6 %collective-permute-start.27 = (bf16[384,1024]{1,0:T(8,128)(2,1)}, bf16[384,1024]{1,0:T(8,128)(2,1)}, u32[]{:S(2)}, u32[]{:S(2)}) collective-permute-start(bf16[384,1024]{1,0:T(8,128)(2,1)} %after.43), channel_id=1, source_target_pairs={{0,1},{1,0},{2,3},{3,2},{4,5},{5,4},{6,7},{7,6},{8,9},{9,8},{10,11... | collective-permute-start | bytes 2359304 | tf_op jit(solution)/shard_map/ppermute | solution.py:66
  356.8 38.9 %collective-permute-start.34 = (bf16[768,256]{1,0:T(8,128)(2,1)S(1)}, bf16[768,256]{1,0:T(8,128)(2,1)}, u32[]{:S(2)}, u32[]{:S(2)}) collective-permute-start(bf16[768,256]{1,0:T(8,128)(2,1)S(1)} %copy-done.66), channel_id=1, source_target_pairs={{0,4},{4,0},{2,6},{6,2},{1,5},{5,1},{3,7},{7,3},{8,12},{12,8},{10,... | collective-permute-start | bytes 1179656 | tf_op jit(solution)/shard_map/ppermute | solution.py:43
  358.8 42.5 %collective-permute-start.35 = (bf16[768,256]{1,0:T(8,128)(2,1)}, bf16[768,256]{1,0:T(8,128)(2,1)}, u32[]{:S(2)}, u32[]{:S(2)}) collective-permute-start(bf16[768,256]{1,0:T(8,128)(2,1)} %add_convert_fusion.13.refs_2_), channel_id=1, source_target_pairs={{0,4},{4,0},{2,6},{6,2},{1,5},{5,1},{3,7},{7,3},{8,12},{12,8},{10,... | collective-permute-start | bytes 1179656 | tf_op jit(solution)/shard_map/ppermute | solution.py:43
  384.1 21.3 %collective-permute-start.36 = (bf16[768,256]{1,0:T(8,128)(2,1)}, bf16[768,256]{1,0:T(8,128)(2,1)}, u32[]{:S(2)}, u32[]{:S(2)}) collective-permute-start(bf16[768,256]{1,0:T(8,128)(2,1)} %add_convert_fusion.12.refs_2_), channel_id=1, source_target_pairs={{0,4},{4,0},{2,6},{6,2},{1,5},{5,1},{3,7},{7,3},{8,12},{12,8},{10,... | collective-permute-start | bytes 1179656 | tf_op jit(solution)/shard_map/ppermute | solution.py:43
  439.3 33.0 %collective-permute-start.41 = (bf16[4,64,2176]{2,1,0:T(8,128)(2,1)}, bf16[4,64,2176]{2,1,0:T(8,128)(2,1)}, u32[]{:S(2)}, u32[]{:S(2)}) collective-permute-start(bf16[4,64,2176]{2,1,0:T(8,128)(2,1)} %dynamic-slice_bitcast_fusion), channel_id=1, source_target_pairs={{0,4},{4,0},{2,6},{6,2},{1,5},{5,1},{3,7},{7,3},{8,12},{12,8},{10,... | collective-permute-start | bytes 3342344 | tf_op jit(solution)/shard_map/ppermute | solution.py:43
  440.9 36.5 %collective-permute-start.39 = (bf16[768,1024]{1,0:T(8,128)(2,1)}, bf16[768,1024]{1,0:T(8,128)(2,1)}, u32[]{:S(2)}, u32[]{:S(2)}) collective-permute-start(bf16[768,1024]{1,0:T(8,128)(2,1)} %get-tuple-element.159), channel_id=1, source_target_pairs={{0,1},{1,0},{2,3},{3,2},{4,5},{5,4},{6,7},{7,6},{8,9},{9,8},{10,11... | collective-permute-start | bytes 4718600 | tf_op jit(solution)/shard_map/ppermute | solution.py:66
  442.9 23.4 %collective-permute-start.48 = (f32[24,128]{1,0:T(8,128)S(1)}, f32[24,128]{1,0:T(8,128)S(1)}, u32[]{:S(2)}, u32[]{:S(2)}) collective-permute-start(f32[24,128]{1,0:T(8,128)S(1)} %fusion.114), channel_id=1, source_target_pairs={{0,4},{4,0},{2,6},{6,2},{1,5},{5,1},{3,7},{7,3},{8,12},{12,8},{10,... | collective-permute-start | bytes 36872 | tf_op jit(solution)/shard_map/ppermute | solution.py:43
  471.0 21.6 %collective-permute-start.50 = (f32[24,128]{1,0:T(8,128)S(1)}, f32[24,128]{1,0:T(8,128)S(1)}, u32[]{:S(2)}, u32[]{:S(2)}) collective-permute-start(f32[24,128]{1,0:T(8,128)S(1)} %add.484), channel_id=1, source_target_pairs={{0,8},{8,0},{16,24},{24,16},{1,9},{9,1},{17,25},{25,17},{2,10},{10... | collective-permute-start | bytes 36872 | tf_op jit(solution)/shard_map/ppermute | solution.py:72
  (122 other events, 832.7 us)
Sparse Core Ops, SparseCore 0:
  68.2 96.0 all-gather.1
  256.3 104.7 reduce-scatter.1

commit v3 on v2

--- a/solution.py
+++ b/solution.py
@@ -17,9 +17,9 @@
 VMEM_LIMIT = 56 * 1024 * 1024
 PAIRS_PER_CALL = 1
 PARTS = 2
-KEY_TILE = 512
+KEY_TILE = 768
 QUERY_TILE = 256
-HIDDEN_TILE = 256
+HIDDEN_TILE = 1024
 WEIGHT = 4
 
 
@@ -516,10 +516,9 @@
         y_parts.append(y_part)
         back_parts.append(back_part)
         mlp_bias_grad = mlp_bias_grad + bias_part
-    d_h2 = [sum_tp(v, y_parts[-1]) for v in back_parts[:-1]]
+    d_h2 = [sum_tp(v, y_parts[-1]) for v in back_parts]
     sides = after(jnp.stack([jnp.concatenate(h2, axis=0), d_down]), *d_h2)
     grads = jnp.einsum("btd,btf->bdf", sides, pair, preferred_element_type=F32).astype(BF)
-    d_h2.append(sum_tp(back_parts[-1], grads))
     grad_mlp = lax.psum_scatter(grads, ("dp", "ctx"), scatter_dimension=1, tiled=True)
     grad_in = grad_mlp[0].astype(F32)
     grad_down = grad_mlp[1].astype(F32).T
@@ -553,7 +552,7 @@
         got = swap_core(send)
         dq, keep = attend_back(query, d_att, attn, lse, (near, over), call, partial)
         if call == calls - 1 and call > 2:
-            got = after(got, result_back)
+            got = after(got, result_back, grad_mlp)
         got = after(got, keep)
         if call == min(1, calls - 1):
             result = give_near(
@@ -571,8 +570,6 @@
         earlier = [mid]
         if call == min(1, calls - 1):
             earlier.append(result[2])
-        if call == min(2, calls - 1):
-            earlier.append(grad_mlp)
     d_kv = [
         (a.astype(F32) + b.astype(F32) + c.astype(F32)).astype(BF) for a, b, c in d_kv
     ]

time: 535 us -> 532 us (level)
  Pallas kernels: 143 us -> 134 us
    pallas_call x2, Pallas kernels: 31 us -> 24.5 us  [mlp(): pl.pallas_call(mlp_kernel, grid=(tiles,), in_specs=[whole, mine, w_in, w_...]
    unnamed x194 -> x188, local copies, waits for them, and re-layouts: 21 us -> 21.1 us
  transfers between devices with their start and end apart: 53 -> 53, of which waited for: 21 -> 22; matrix products, arithmetic and copies ran while one was open for 21% -> 21% of each run, Pallas kernels for 27% -> 26%
where the time goes in v3:
time: 532 us; the launch traced here: 526 us
  waiting for transfers between devices  152 us (29%)
  Pallas kernels  134 us (25%)
  other arithmetic  81.4 us (15%)
  matrix products  54.9 us (10%)
  local copies, waits for them, and re-layouts  42.8 us (8%)
  starting transfers between devices  38.4 us (7%)
  between operations  22.4 us (4%)
    ppermute x15, waiting for transfers between devices, swap_y(): return lax.ppermute(v, 'ctx', [(0, 2), (2, 0), (1, 3), (3, 1)])  78.4 us
    pallas_call x8, Pallas kernels, attend_back(): pl.pallas_call(functools.partial(attend_back_kernel, LOG2E / math.sqrt(HD...  70.9 us
    pallas_call x4, Pallas kernels, attend(): pl.pallas_call(functools.partial(attend_kernel, LOG2E / math.sqrt(HD)), g...  38.8 us
    ppermute x7, waiting for transfers between devices, sum_tp(): other = after(lax.ppermute(part, 'tp', [(0, 1), (1, 0)]), *earlier)  36.7 us
    pallas_call x2, Pallas kernels, mlp(): pl.pallas_call(mlp_kernel, grid=(tiles,), in_specs=[whole, mine, w_in, w_...  24.5 us
    ppermute x6, waiting for transfers between devices, swap_line(): lax.ppermute(v, 'dp', [(i, i ^ bit) for i in range(lax.axis_size('dp'))])  23.8 us
    dot_general x9, matrix products, dot_nn(): return jnp.dot(a, b, preferred_element_type=F32)  22.5 us
    unnamed x188, local copies, waits for them, and re-layouts  21.1 us
  transfers between devices with their start and end apart: 53, of which 22 were waited for; matrix products, arithmetic and copies ran while one was open for 21% of the time, Pallas kernels for 26%

profile of v3, /device:TPU:0, one launch (start us, length us, event | category | flops | bytes accessed | tf_op | source)
XLA Modules:
  0.0 525.9 jit_solution(1946265810274772183)
XLA Ops:
  30.6 10.5 %collective-permute-done.4 = bf16[2,64,1664]{2,1,0:T(8,128)(2,1)S(1)} collective-permute-done((bf16[2,64,1664]{2,1,0:T(8,128)(2,1)}, bf16[2,64,1664]{2,1,0:T(8,128)(2,1)S(1)}, u32[]{:S(2)}, u32[]{:S(2)}) %collective-permute-start.4) | collective-permute-done | bytes 426016 | tf_op jit(solution)/shard_map/ppermute | solution.py:72
  50.1 17.7 %collective-permute-done.5.refs_1_ = bf16[4,64,1664]{2,1,0:T(8,128)(2,1)S(1)} collective-permute-done((bf16[4,64,1664]{2,1,0:T(8,128)(2,1)}, bf16[4,64,1664]{2,1,0:T(8,128)(2,1)S(1)}, u32[]{:S(2)}, u32[]{:S(2)}) %collective-permute-start.5) | collective-permute-done | bytes 852000 | tf_op jit(solution)/shard_map/ppermute | solution.py:43
  80.5 13.5 %collective-permute-done.8.refs_1_.k1 = bf16[768,256]{1,0:T(8,128)(2,1)} collective-permute-done((bf16[768,256]{1,0:T(8,128)(2,1)}, bf16[768,256]{1,0:T(8,128)(2,1)}, u32[]{:S(2)}, u32[]{:S(2)}) %collective-permute-start.8) | collective-permute-done | bytes 393248 | tf_op jit(solution)/shard_map/ppermute | solution.py:43
  99.0 9.6 %attend.4 = (f32[768,512]{1,0:T(8,128)}, bf16[768,512]{1,0:T(8,128)(2,1)}, f32[4,8,768]{2,1,0:T(8,128)}) custom-call(bf16[768,512]{1,0:T(8,128)(2,1)} %add_convert_fusion.6.q_ref, bf16[768,256]{1,0:T(8,128)(2,1)} %fusion.46.k0.refs_0_, bf16[768,256]{1,0:T(8,128)(2,1)} %collective-permute-done.8.refs_1_.k1, ...), custom_call_target="tpu_custom_call" | custom-call | flops 1207959552 | bytes 393216 | tf_op jit(solution)/shard_map/attend/pallas_call | solution.py:194
  117.5 9.6 %attend.5 = (f32[768,512]{1,0:T(8,128)}, bf16[768,512]{1,0:T(8,128)(2,1)}, f32[4,8,768]{2,1,0:T(8,128)}) custom-call(bf16[768,512]{1,0:T(8,128)(2,1)} %add_convert_fusion.6.q_ref, bf16[768,256]{1,0:T(8,128)(2,1)} %after.30.k0.refs_0_, bf16[768,256]{1,0:T(8,128)(2,1)} %after.31.k1.refs_1_, ...), custom_call_target="tpu_custom_call", output_to_operand_aliasing={{0}: (5, {}), {1}: (6, {}), {2}: (7, {})} | custom-call | flops 1207959552 | bytes 393216 | tf_op jit(solution)/shard_map/attend/pallas_call | solution.py:194
  135.8 13.4 %collective-permute-done.14.refs_0_.refs_1_ = bf16[768,256]{1,0:T(8,128)(2,1)S(1)} collective-permute-done((bf16[768,256]{1,0:T(8,128)(2,1)}, bf16[768,256]{1,0:T(8,128)(2,1)S(1)}, u32[]{:S(2)}, u32[]{:S(2)}) %collective-permute-start.14) | collective-permute-done | bytes 393248 | tf_op jit(solution)/shard_map/ppermute | solution.py:43
  150.3 9.9 %attend.6 = (f32[768,512]{1,0:T(8,128)}, bf16[768,512]{1,0:T(8,128)(2,1)}, f32[4,8,768]{2,1,0:T(8,128)}) custom-call(bf16[768,512]{1,0:T(8,128)(2,1)} %add_convert_fusion.6.q_ref, bf16[768,256]{1,0:T(8,128)(2,1)} %after.33.k0.refs_0_, bf16[768,256]{1,0:T(8,128)(2,1)} %after.34.k1.refs_1_, ...), custom_call_target="tpu_custom_call", output_to_operand_aliasing={{0}: (5, {}), {1}: (6, {}), {2}: (7, {})} | custom-call | flops 1207959552 | bytes 393216 | tf_op jit(solution)/shard_map/attend/pallas_call | solution.py:194
  163.3 9.7 %attend.7 = (f32[768,512]{1,0:T(8,128)}, bf16[768,512]{1,0:T(8,128)(2,1)}, f32[4,8,768]{2,1,0:T(8,128)}) custom-call(bf16[768,512]{1,0:T(8,128)(2,1)} %add_convert_fusion.6.q_ref, bf16[768,256]{1,0:T(8,128)(2,1)} %after.32.k0.refs_0_, bf16[768,256]{1,0:T(8,128)(2,1)} %after.35.k1.refs_1_, ...), custom_call_target="tpu_custom_call", output_to_operand_aliasing={{0}: (5, {}), {1}: (6, {}), {2}: (7, {})} | custom-call | flops 1207959552 | bytes 393216 | tf_op jit(solution)/shard_map/attend/pallas_call | solution.py:194
  186.5 12.2 %collective-permute-done.20 = bf16[384,1024]{1,0:T(8,128)(2,1)S(1)} collective-permute-done((bf16[384,1024]{1,0:T(8,128)(2,1)S(1)}, bf16[384,1024]{1,0:T(8,128)(2,1)S(1)}, u32[]{:S(2)}, u32[]{:S(2)}) %collective-permute-start.20) | collective-permute-done | bytes 786464 | tf_op jit(solution)/shard_map/ppermute | solution.py:66
  200.6 12.3 %mlp.2 = (bf16[2,768,2048]{2,1,0:T(8,128)(2,1)}, bf16[384,1024]{1,0:T(8,128)(2,1)}, bf16[384,1024]{1,0:T(8,128)(2,1)}, f32[1,2048]{1,0:T(1,128)}) custom-call(bf16[384,1024]{1,0:T(8,128)(2,1)} %add_convert_fusion.5.h2_ref, bf16[768,1024]{1,0:T(8,128)(2,1)} %get-tuple-element.215.d_ref, bf16[1024,4608]{1,0:T(8,128)(2,1)} %all-gather.2.cloned.1.call-done.in_ref.down_ref, ...), custom_call_target="tpu_custom_call" | custom-call | flops 1610612736 | bytes 3670016 | tf_op jit(solution)/shard_map/mlp/pallas_call | solution.py:356
  219.8 12.2 %mlp.3 = (bf16[2,768,2048]{2,1,0:T(8,128)(2,1)}, bf16[384,1024]{1,0:T(8,128)(2,1)}, bf16[384,1024]{1,0:T(8,128)(2,1)}, f32[1,2048]{1,0:T(1,128)}) custom-call(bf16[384,1024]{1,0:T(8,128)(2,1)} %add_convert_fusion.4.h2_ref, bf16[768,1024]{1,0:T(8,128)(2,1)} %get-tuple-element.215.d_ref, ...), custom_call_target="tpu_custom_call", output_to_operand_aliasing={{0}: (5, {})} | custom-call | flops 1610612736 | bytes 3670016 | tf_op jit(solution)/shard_map/mlp/pallas_call | solution.py:356
  235.8 15.5 %collective-permute-done.26.refs_0_ = bf16[384,1024]{1,0:T(8,128)(2,1)} collective-permute-done((bf16[384,1024]{1,0:T(8,128)(2,1)}, bf16[384,1024]{1,0:T(8,128)(2,1)}, u32[]{:S(2)}, u32[]{:S(2)}) %collective-permute-start.26) | collective-permute-done | bytes 786464 | tf_op jit(solution)/shard_map/ppermute | solution.py:66
  259.9 12.7 %convolution_convert_fusion.refs_2_ = bf16[2,1024,2048]{2,1,0:T(8,128)(2,1)} fusion(bf16[2,768,1024]{2,1,0:T(8,128)(2,1)} %after.43, bf16[2,768,2048]{2,1,0:T(8,128)(2,1)} %get-tuple-element.64), kind=kOutput, calls=%fused_computation | convolution fusion | flops 6446645248 | bytes 17825792 | tf_op jit(solution)/shard_map/btd,btf->bdf/dot_general | solution.py:521
  277.7 8.7 %attend_back.8 = (f32[128,768]{1,0:T(8,128)}, bf16[1536,256]{1,0:T(8,128)(2,1)}) custom-call(bf16[768,512]{1,0:T(8,128)(2,1)} %add_convert_fusion.6.q_ref, bf16[768,512]{1,0:T(8,128)(2,1)} %pad_maximum_fusion.7.refs_1_.d_ref, f32[768,512]{1,0:T(8,128)} %get-tuple-element.63.o_ref, f32[4,8,768]{2,1,0:T(8,128)} %get-tuple-element.57.refs_1_.lse_ref, ...), custom_call_target="tpu_custom_call" | custom-call | flops 1509949440 | bytes 983040 | tf_op jit(solution)/shard_map/attend_back/pallas_call | solution.py:280
  290.0 8.9 %attend_back.9 = (bf16[768,128]{1,0:T(8,128)(2,1)}, bf16[1536,256]{1,0:T(8,128)(2,1)}) custom-call(bf16[768,512]{1,0:T(8,128)(2,1)} %add_convert_fusion.6.q_ref, bf16[768,512]{1,0:T(8,128)(2,1)} %pad_maximum_fusion.7.refs_1_.d_ref, f32[768,512]{1,0:T(8,128)} %get-tuple-element.63.o_ref, f32[4,8,768]{2,1,0:T(8,128)} %get-tuple-element.57.refs_1_.lse_ref, ...), custom_call_target="tpu_custom_call" | custom-call | flops 1509949440 | bytes 983040 | tf_op jit(solution)/shard_map/attend_back/pallas_call | solution.py:280
  300.9 8.8 %attend_back.10 = (f32[128,768]{1,0:T(8,128)}, bf16[1536,256]{1,0:T(8,128)(2,1)}) custom-call(bf16[768,512]{1,0:T(8,128)(2,1)} %add_convert_fusion.6.q_ref, bf16[768,512]{1,0:T(8,128)(2,1)} %pad_maximum_fusion.7.refs_1_.d_ref, f32[768,512]{1,0:T(8,128)} %get-tuple-element.63.o_ref, f32[4,8,768]{2,1,0:T(8,128)} %get-tuple-element.57.refs_1_.lse_ref, ...), custom_call_target="tpu_custom_call" | custom-call | flops 1509949440 | bytes 983040 | tf_op jit(solution)/shard_map/attend_back/pallas_call | solution.py:280
  309.7 8.7 %attend_back.11 = (bf16[768,128]{1,0:T(8,128)(2,1)}, bf16[1536,256]{1,0:T(8,128)(2,1)}) custom-call(bf16[768,512]{1,0:T(8,128)(2,1)} %add_convert_fusion.6.q_ref, bf16[768,512]{1,0:T(8,128)(2,1)} %pad_maximum_fusion.7.refs_1_.d_ref, f32[768,512]{1,0:T(8,128)} %get-tuple-element.63.o_ref, f32[4,8,768]{2,1,0:T(8,128)} %get-tuple-element.57.refs_1_.lse_ref, ...), custom_call_target="tpu_custom_call" | custom-call | flops 1509949440 | bytes 983040 | tf_op jit(solution)/shard_map/attend_back/pallas_call | solution.py:280
  336.8 9.1 %attend_back.12 = (f32[128,768]{1,0:T(8,128)}, bf16[1536,256]{1,0:T(8,128)(2,1)}) custom-call(bf16[768,512]{1,0:T(8,128)(2,1)} %add_convert_fusion.6.q_ref, bf16[768,512]{1,0:T(8,128)(2,1)} %pad_maximum_fusion.7.refs_1_.d_ref, f32[768,512]{1,0:T(8,128)} %get-tuple-element.63.o_ref, f32[4,8,768]{2,1,0:T(8,128)} %get-tuple-element.57.refs_1_.lse_ref, ...), custom_call_target="tpu_custom_call" | custom-call | flops 1509949440 | bytes 983040 | tf_op jit(solution)/shard_map/attend_back/pallas_call | solution.py:280
  354.1 8.7 %attend_back.13 = (bf16[768,128]{1,0:T(8,128)(2,1)}, bf16[1536,256]{1,0:T(8,128)(2,1)}) custom-call(bf16[768,512]{1,0:T(8,128)(2,1)} %add_convert_fusion.6.q_ref, bf16[768,512]{1,0:T(8,128)(2,1)} %pad_maximum_fusion.7.refs_1_.d_ref, f32[768,512]{1,0:T(8,128)} %get-tuple-element.63.o_ref, f32[4,8,768]{2,1,0:T(8,128)} %get-tuple-element.57.refs_1_.lse_ref, ...), custom_call_target="tpu_custom_call" | custom-call | flops 1509949440 | bytes 983040 | tf_op jit(solution)/shard_map/attend_back/pallas_call | solution.py:280
  366.1 8.8 %attend_back.14 = (f32[128,768]{1,0:T(8,128)}, bf16[1536,256]{1,0:T(8,128)(2,1)}) custom-call(bf16[768,512]{1,0:T(8,128)(2,1)} %add_convert_fusion.6.q_ref, bf16[768,512]{1,0:T(8,128)(2,1)} %pad_maximum_fusion.7.refs_1_.d_ref, f32[768,512]{1,0:T(8,128)} %get-tuple-element.63.o_ref, f32[4,8,768]{2,1,0:T(8,128)} %get-tuple-element.57.refs_1_.lse_ref, ...), custom_call_target="tpu_custom_call" | custom-call | flops 1509949440 | bytes 983040 | tf_op jit(solution)/shard_map/attend_back/pallas_call | solution.py:280
  378.9 9.1 %attend_back.15 = (bf16[768,128]{1,0:T(8,128)(2,1)}, bf16[1536,256]{1,0:T(8,128)(2,1)}) custom-call(bf16[768,512]{1,0:T(8,128)(2,1)} %add_convert_fusion.6.q_ref, bf16[768,512]{1,0:T(8,128)(2,1)} %pad_maximum_fusion.7.refs_1_.d_ref, f32[768,512]{1,0:T(8,128)} %get-tuple-element.63.o_ref, f32[4,8,768]{2,1,0:T(8,128)} %get-tuple-element.57.refs_1_.lse_ref, ...), custom_call_target="tpu_custom_call" | custom-call | flops 1509949440 | bytes 983040 | tf_op jit(solution)/shard_map/attend_back/pallas_call | solution.py:280
  408.5 6.6 %fusion.114 = (bf16[1024]{0:T(1024)(128)(2,1)S(1)}, bf16[1024]{0:T(1024)(128)(2,1)S(1)}, bf16[768,1024]{1,0:T(8,128)(2,1)}) fusion(f32[768]{0:T(1024)S(1)} %add_rsqrt_fusion, f32[768]{0:T(1024)S(1)} %broadcast_multiply_fusion.2, bf16[768,1024]{1,0:T(8,128)(2,1)S(1)} %copy-done.1, bf16[768,1536]{1,0:T(8,128)(2,1)} %fusion.72, bf16[1024,1664]{1,0:T(8,128)(2,1)} %bitcast.149), kind=kOutput, calls=%fused_computation.249 | convolution fusion | flops 2421422080 | bytes 8660992 | tf_op jit(solution)/shard_map/dot_general | solution.py:27
  439.6 21.7 %collective-permute-done.48 = f32[24,128]{1,0:T(8,128)S(1)} collective-permute-done((f32[24,128]{1,0:T(8,128)S(1)}, f32[24,128]{1,0:T(8,128)S(1)}, u32[]{:S(2)}, u32[]{:S(2)}) %collective-permute-start.48) | collective-permute-done | bytes 12320 | tf_op jit(solution)/shard_map/ppermute | solution.py:43
  497.7 9.4 %collective-permute-done.45.refs_0_ = bf16[1,64,2176]{2,1,0:T(8,128)(2,1)S(1)} collective-permute-done((bf16[1,64,2176]{2,1,0:T(8,128)(2,1)S(1)}, bf16[1,64,2176]{2,1,0:T(8,128)(2,1)S(1)}, u32[]{:S(2)}, u32[]{:S(2)}) %collective-permute-start.45) | collective-permute-done | bytes 278560 | tf_op jit(solution)/shard_map/ppermute | solution.py:72
  (459 shorter events, 235.9 us)
Async XLA Ops:
  7.2 169.1 %all-gather.2.cloned.1.call-start = ((), (), s32[]{:S(2)}) async-start(), calls=%async_computation.1 | async-start | bytes 10027008 | tf_op jit(solution)/shard_map/all_gather | solution.py:473
  8.3 19.8 %collective-permute-start = (bf16[256,1024]{1,0:T(8,128)(2,1)S(1)}, bf16[256,1024]{1,0:T(8,128)(2,1)S(1)}, u32[]{:S(2)}, u32[]{:S(2)}) collective-permute-start(bf16[256,1024]{1,0:T(8,128)(2,1)S(1)} %slice_bitcast_fusion.1), channel_id=1, source_target_pairs={{0,4},{4,0},{2,6},{6,2},{1,5},{5,1},{3,7},{7,3},{8,12},{12,8},{10,... | collective-permute-start | bytes 1572872 | tf_op jit(solution)/shard_map/ppermute | solution.py:43
  11.3 31.9 %collective-permute-start.1 = (bf16[256,1024]{1,0:T(8,128)(2,1)S(1)}, bf16[256,1024]{1,0:T(8,128)(2,1)S(1)}, u32[]{:S(2)}, u32[]{:S(2)}) collective-permute-start(bf16[256,1024]{1,0:T(8,128)(2,1)S(1)} %slice_bitcast_fusion.1), channel_id=1, source_target_pairs={{0,2},{2,0},{4,6},{6,4},{1,3},{3,1},{5,7},{7,5},{8,10},{10,8},{12,... | collective-permute-start | bytes 1572872 | tf_op jit(solution)/shard_map/ppermute | solution.py:39
  47.3 20.5 %collective-permute-start.5 = (bf16[4,64,1664]{2,1,0:T(8,128)(2,1)}, bf16[4,64,1664]{2,1,0:T(8,128)(2,1)S(1)}, u32[]{:S(2)}, u32[]{:S(2)}) collective-permute-start(bf16[4,64,1664]{2,1,0:T(8,128)(2,1)} %after.29), channel_id=1, source_target_pairs={{0,4},{4,0},{2,6},{6,2},{1,5},{5,1},{3,7},{7,3},{8,12},{12,8},{10,... | collective-permute-start | bytes 2555912 | tf_op jit(solution)/shard_map/ppermute | solution.py:43
  68.7 323.1 %reduce-scatter.2.cloned.1.call-start = ((), (), s32[]{:S(2)}) async-start(), calls=%async_computation.2 | async-start | bytes 8912896 | tf_op jit(solution)/shard_map/reduce_scatter | solution.py:522
  112.0 20.6 %collective-permute-start.15 = (bf16[768,256]{1,0:T(8,128)(2,1)}, bf16[768,256]{1,0:T(8,128)(2,1)S(1)}, u32[]{:S(2)}, u32[]{:S(2)}) collective-permute-start(bf16[768,256]{1,0:T(8,128)(2,1)} %after.33.k0.refs_0_), channel_id=1, source_target_pairs={{0,4},{4,0},{2,6},{6,2},{1,5},{5,1},{3,7},{7,3},{8,12},{12,8},{10,... | collective-permute-start | bytes 1179656 | tf_op jit(solution)/shard_map/ppermute | solution.py:43
  127.1 22.0 %collective-permute-start.14 = (bf16[768,256]{1,0:T(8,128)(2,1)}, bf16[768,256]{1,0:T(8,128)(2,1)S(1)}, u32[]{:S(2)}, u32[]{:S(2)}) collective-permute-start(bf16[768,256]{1,0:T(8,128)(2,1)} %after.32.k0.refs_0_), channel_id=1, source_target_pairs={{0,4},{4,0},{2,6},{6,2},{1,5},{5,1},{3,7},{7,3},{8,12},{12,8},{10,... | collective-permute-start | bytes 1179656 | tf_op jit(solution)/shard_map/ppermute | solution.py:43
  127.4 22.8 %collective-permute-start.16 = (bf16[768,256]{1,0:T(8,128)(2,1)}, bf16[768,256]{1,0:T(8,128)(2,1)}, u32[]{:S(2)}, u32[]{:S(2)}) collective-permute-start(bf16[768,256]{1,0:T(8,128)(2,1)} %after.33.k0.refs_0_), channel_id=1, source_target_pairs={{0,2},{2,0},{4,6},{6,4},{1,3},{3,1},{5,7},{7,5},{8,10},{10,8},{12,... | collective-permute-start | bytes 1179656 | tf_op jit(solution)/shard_map/ppermute | solution.py:39
  135.2 25.4 %collective-permute-start.18 = (bf16[768,256]{1,0:T(8,128)(2,1)S(1)}, bf16[768,256]{1,0:T(8,128)(2,1)}, u32[]{:S(2)}, u32[]{:S(2)}) collective-permute-start(bf16[768,256]{1,0:T(8,128)(2,1)S(1)} %copy-done.51), channel_id=1, source_target_pairs={{0,2},{2,0},{4,6},{6,4},{1,3},{3,1},{5,7},{7,5},{8,10},{10,8},{12,... | collective-permute-start | bytes 1179656 | tf_op jit(solution)/shard_map/ppermute | solution.py:39
  149.9 23.1 %collective-permute-start.21 = (bf16[256,1024]{1,0:T(8,128)(2,1)}, bf16[256,1024]{1,0:T(8,128)(2,1)S(1)}, u32[]{:S(2)}, u32[]{:S(2)}) collective-permute-start(bf16[256,1024]{1,0:T(8,128)(2,1)} %after.37), channel_id=1, source_target_pairs={{0,4},{4,0},{2,6},{6,2},{1,5},{5,1},{3,7},{7,3},{8,12},{12,8},{10,... | collective-permute-start | bytes 1572872 | tf_op jit(solution)/shard_map/ppermute | solution.py:43
  160.1 19.8 %collective-permute-start.22 = (bf16[256,1024]{1,0:T(8,128)(2,1)S(1)}, bf16[256,1024]{1,0:T(8,128)(2,1)}, u32[]{:S(2)}, u32[]{:S(2)}) collective-permute-start(bf16[256,1024]{1,0:T(8,128)(2,1)S(1)} %slice_bitcast_fusion), channel_id=1, source_target_pairs={{0,2},{2,0},{4,6},{6,4},{1,3},{3,1},{5,7},{7,5},{8,10},{10,8},{12,... | collective-permute-start | bytes 1572872 | tf_op jit(solution)/shard_map/ppermute | solution.py:39
  178.3 20.4 %collective-permute-start.20 = (bf16[384,1024]{1,0:T(8,128)(2,1)S(1)}, bf16[384,1024]{1,0:T(8,128)(2,1)S(1)}, u32[]{:S(2)}, u32[]{:S(2)}) collective-permute-start(bf16[384,1024]{1,0:T(8,128)(2,1)S(1)} %convolution_convert_fusion.4), channel_id=1, source_target_pairs={{0,1},{1,0},{2,3},{3,2},{4,5},{5,4},{6,7},{7,6},{8,9},{9,8},{10,11... | collective-permute-start | bytes 2359304 | tf_op jit(solution)/shard_map/ppermute | solution.py:66
  186.0 29.0 %collective-permute-start.25 = (bf16[384,1024]{1,0:T(8,128)(2,1)S(1)}, bf16[384,1024]{1,0:T(8,128)(2,1)S(1)}, u32[]{:S(2)}, u32[]{:S(2)}) collective-permute-start(bf16[384,1024]{1,0:T(8,128)(2,1)S(1)} %convolution_convert_fusion.3), channel_id=1, source_target_pairs={{0,1},{1,0},{2,3},{3,2},{4,5},{5,4},{6,7},{7,6},{8,9},{9,8},{10,11... | collective-permute-start | bytes 2359304 | tf_op jit(solution)/shard_map/ppermute | solution.py:66
  213.0 22.8 %collective-permute-start.24 = (bf16[384,1024]{1,0:T(8,128)(2,1)}, bf16[384,1024]{1,0:T(8,128)(2,1)}, u32[]{:S(2)}, u32[]{:S(2)}) collective-permute-start(bf16[384,1024]{1,0:T(8,128)(2,1)} %get-tuple-element.59), channel_id=1, source_target_pairs={{0,1},{1,0},{2,3},{3,2},{4,5},{5,4},{6,7},{7,6},{8,9},{9,8},{10,11... | collective-permute-start | bytes 2359304 | tf_op jit(solution)/shard_map/ppermute | solution.py:66
  232.0 19.2 %collective-permute-start.26 = (bf16[384,1024]{1,0:T(8,128)(2,1)}, bf16[384,1024]{1,0:T(8,128)(2,1)}, u32[]{:S(2)}, u32[]{:S(2)}) collective-permute-start(bf16[384,1024]{1,0:T(8,128)(2,1)} %get-tuple-element.62), channel_id=1, source_target_pairs={{0,1},{1,0},{2,3},{3,2},{4,5},{5,4},{6,7},{7,6},{8,9},{9,8},{10,11... | collective-permute-start | bytes 2359304 | tf_op jit(solution)/shard_map/ppermute | solution.py:66
  286.5 31.9 %collective-permute-start.27 = (bf16[384,1024]{1,0:T(8,128)(2,1)}, bf16[384,1024]{1,0:T(8,128)(2,1)}, u32[]{:S(2)}, u32[]{:S(2)}) collective-permute-start(bf16[384,1024]{1,0:T(8,128)(2,1)} %after.42), channel_id=1, source_target_pairs={{0,1},{1,0},{2,3},{3,2},{4,5},{5,4},{6,7},{7,6},{8,9},{9,8},{10,11... | collective-permute-start | bytes 2359304 | tf_op jit(solution)/shard_map/ppermute | solution.py:66
  288.1 35.5 %collective-permute-start.29 = (bf16[384,1024]{1,0:T(8,128)(2,1)}, bf16[384,1024]{1,0:T(8,128)(2,1)}, u32[]{:S(2)}, u32[]{:S(2)}) collective-permute-start(bf16[384,1024]{1,0:T(8,128)(2,1)} %after.46), channel_id=1, source_target_pairs={{0,1},{1,0},{2,3},{3,2},{4,5},{5,4},{6,7},{7,6},{8,9},{9,8},{10,11... | collective-permute-start | bytes 2359304 | tf_op jit(solution)/shard_map/ppermute | solution.py:66
  350.8 38.9 %collective-permute-start.34 = (bf16[768,256]{1,0:T(8,128)(2,1)S(1)}, bf16[768,256]{1,0:T(8,128)(2,1)}, u32[]{:S(2)}, u32[]{:S(2)}) collective-permute-start(bf16[768,256]{1,0:T(8,128)(2,1)S(1)} %copy-done.65), channel_id=1, source_target_pairs={{0,4},{4,0},{2,6},{6,2},{1,5},{5,1},{3,7},{7,3},{8,12},{12,8},{10,... | collective-permute-start | bytes 1179656 | tf_op jit(solution)/shard_map/ppermute | solution.py:43
  354.1 42.4 %collective-permute-start.35 = (bf16[768,256]{1,0:T(8,128)(2,1)}, bf16[768,256]{1,0:T(8,128)(2,1)}, u32[]{:S(2)}, u32[]{:S(2)}) collective-permute-start(bf16[768,256]{1,0:T(8,128)(2,1)} %add_convert_fusion.13.refs_2_), channel_id=1, source_target_pairs={{0,4},{4,0},{2,6},{6,2},{1,5},{5,1},{3,7},{7,3},{8,12},{12,8},{10,... | collective-permute-start | bytes 1179656 | tf_op jit(solution)/shard_map/ppermute | solution.py:43
  378.9 20.6 %collective-permute-start.36 = (bf16[768,256]{1,0:T(8,128)(2,1)}, bf16[768,256]{1,0:T(8,128)(2,1)}, u32[]{:S(2)}, u32[]{:S(2)}) collective-permute-start(bf16[768,256]{1,0:T(8,128)(2,1)} %add_convert_fusion.12.refs_2_), channel_id=1, source_target_pairs={{0,4},{4,0},{2,6},{6,2},{1,5},{5,1},{3,7},{7,3},{8,12},{12,8},{10,... | collective-permute-start | bytes 1179656 | tf_op jit(solution)/shard_map/ppermute | solution.py:43
  434.3 32.5 %collective-permute-start.41 = (bf16[4,64,2176]{2,1,0:T(8,128)(2,1)}, bf16[4,64,2176]{2,1,0:T(8,128)(2,1)}, u32[]{:S(2)}, u32[]{:S(2)}) collective-permute-start(bf16[4,64,2176]{2,1,0:T(8,128)(2,1)} %dynamic-slice_bitcast_fusion), channel_id=1, source_target_pairs={{0,4},{4,0},{2,6},{6,2},{1,5},{5,1},{3,7},{7,3},{8,12},{12,8},{10,... | collective-permute-start | bytes 3342344 | tf_op jit(solution)/shard_map/ppermute | solution.py:43
  436.5 36.5 %collective-permute-start.39 = (bf16[768,1024]{1,0:T(8,128)(2,1)}, bf16[768,1024]{1,0:T(8,128)(2,1)}, u32[]{:S(2)}, u32[]{:S(2)}) collective-permute-start(bf16[768,1024]{1,0:T(8,128)(2,1)} %get-tuple-element.159), channel_id=1, source_target_pairs={{0,1},{1,0},{2,3},{3,2},{4,5},{5,4},{6,7},{7,6},{8,9},{9,8},{10,11... | collective-permute-start | bytes 4718600 | tf_op jit(solution)/shard_map/ppermute | solution.py:66
  439.3 22.0 %collective-permute-start.48 = (f32[24,128]{1,0:T(8,128)S(1)}, f32[24,128]{1,0:T(8,128)S(1)}, u32[]{:S(2)}, u32[]{:S(2)}) collective-permute-start(f32[24,128]{1,0:T(8,128)S(1)} %fusion.111), channel_id=1, source_target_pairs={{0,4},{4,0},{2,6},{6,2},{1,5},{5,1},{3,7},{7,3},{8,12},{12,8},{10,... | collective-permute-start | bytes 36872 | tf_op jit(solution)/shard_map/ppermute | solution.py:43
  466.0 21.2 %collective-permute-start.50 = (f32[24,128]{1,0:T(8,128)S(1)}, f32[24,128]{1,0:T(8,128)S(1)}, u32[]{:S(2)}, u32[]{:S(2)}) collective-permute-start(f32[24,128]{1,0:T(8,128)S(1)} %add.484), channel_id=1, source_target_pairs={{0,8},{8,0},{16,24},{24,16},{1,9},{9,1},{17,25},{25,17},{2,10},{10... | collective-permute-start | bytes 36872 | tf_op jit(solution)/shard_map/ppermute | solution.py:72
  (119 other events, 840.3 us)
Sparse Core Ops, SparseCore 0:
  68.9 98.5 all-gather.1
  272.7 111.2 reduce-scatter.1
